TPU v7x, 512 devices: a whole 4x8x8 slice. The times are simulated.
512 devices in a mesh: tm: 8 (over x, core), space: 64 (over y, z).
Axes of the slice: x: 4, y: 8, z: 8, core: 2. Of those that a mesh axis runs over, the one named last changes fastest.
Arguments:
- ensemble: bfloat16 [16, 131072, 256], P('tm', 'space'), may hold values from -6 to 6
- obs_index: int32 [16, 32768], P('tm', 'space'), may hold values from 0 to 2047
- obs_value: float32 [16, 32768], P('tm', 'space'), may hold values from -48 to 48
- obs_var: float32 [16, 32768], P('tm', 'space'), may hold values from 256 to 2048
Outputs:
- smoothed: bfloat16 [16, 131072, 256], P('tm', 'space')
All inputs are finite; a program needn't handle non-finite values.
Results may differ from a plain program's by a relative error of at most 0.0049.
Values sent between devices are 32-bit elements; how exact they have to be, the bound alone decides.
A program may use at most 64 MiB of HBM per device.

v0:
```python
import jax
import jax.numpy as jnp
from jax import lax
from jax.sharding import PartitionSpec as P

NS_ITERS = 6


HIGH = lax.Precision.HIGHEST


def passed_along(array, axis, by):
    size = lax.axis_size(axis)
    pairs = [(i, i + by) for i in range(size) if 0 <= i + by < size]
    return lax.ppermute(array, axis, pairs)


def partial_sums(rows, value, var):
    mean = jnp.mean(rows, axis=1, keepdims=True)
    anom = rows - mean
    innov = value - mean[:, 0]
    inv_var = 1.0 / var
    gram = jnp.dot(anom.T, anom * inv_var[:, None], precision=HIGH)
    proj = jnp.dot(innov * inv_var, anom, precision=HIGH)
    return (gram, proj)


def finish_transform(gram, proj):
    width = gram.shape[0]
    eye = jnp.eye(width, dtype=jnp.float32)
    amat = (width - 1.0) * eye + gram
    scale = jnp.sqrt(jnp.sum(amat * amat))
    ycur = amat / scale
    zcur = eye
    for step in range(NS_ITERS):
        tmat = 1.5 * eye - 0.5 * jnp.dot(zcur, ycur, precision=HIGH)
        ycur = jnp.dot(ycur, tmat, precision=HIGH)
        zcur = jnp.dot(tmat, zcur, precision=HIGH)
    wmean = jnp.dot(zcur, jnp.dot(zcur, proj, precision=HIGH), precision=HIGH) / scale
    wtrans = jnp.sqrt(width - 1.0) * zcur / jnp.sqrt(scale)
    qmat = wmean[:, None] + wtrans
    return qmat - jnp.mean(qmat, axis=0, keepdims=True) + 1.0 / width


def on_device(ensemble, obs_index, obs_value, obs_var):
    windows_here = ensemble.shape[0]
    width = ensemble.shape[2]
    grams = []
    projs = []
    for w in range(windows_here):
        rows = jnp.take(ensemble[w], obs_index[w], axis=0).astype(jnp.float32)
        gram, proj = partial_sums(rows, obs_value[w], obs_var[w])
        grams.append(gram)
        projs.append(proj)
    gram_all, proj_all = lax.psum((jnp.stack(grams), jnp.stack(projs)), "space")
    gmats = [finish_transform(gram_all[w], proj_all[w]) for w in range(windows_here)]
    eye = jnp.eye(width, dtype=jnp.float32)
    local_prod = gmats[windows_here - 1]
    w = 0
    local_prod = jnp.dot(gmats[w], local_prod, precision=HIGH)
    is_last = lax.axis_index("tm") == lax.axis_size("tm") - 1
    later = eye
    for step in range(lax.axis_size("tm") - 1):
        moved = passed_along(jnp.dot(local_prod, later, precision=HIGH), "tm", -1)
        later = jnp.where(is_last, eye, moved)
    results = [None] * windows_here
    suffix = later
    for w in range(windows_here - 1, -1, -1):
        suffix = jnp.dot(gmats[w], suffix, precision=HIGH)
        results[w] = jnp.dot(
            ensemble[w], suffix.astype(jnp.bfloat16), preferred_element_type=jnp.float32
        ).astype(jnp.bfloat16)
    return jnp.stack(results)


def solution(mesh):
    placed = (P("tm", "space", None), P("tm", "space"), P("tm", "space"), P("tm", "space"))
    return jax.shard_map(
        on_device, mesh=mesh, in_specs=placed, out_specs=P("tm", "space", None), check_vma=False
    )
```

profile of v0, /device:TPU:1, one launch (start us, length us, event | category | flops | bytes accessed | tf_op | source)
XLA Modules:
  0.0 267.9 jit_solution(13143895297095381743)
XLA Ops:
  6.5 0.8 fusion.60
  7.4 0.8 fusion.59
  8.1 0.8 slice_divide_fusion.1
  8.9 1.7 slice_bitcast_fusion.1
  10.6 2.0 gather_fusion
  12.8 1.4 convolution_bitcast_fusion.1
  14.2 2.0 gather_fusion.1
  16.4 1.4 convolution_bitcast_fusion
  17.8 0.8 pad_maximum_fusion.1
  19.6 123.5 %psum.15 = f32[2,256]{1,0:T(2,128)S(1)} all-reduce(f32[2,256]{1,0:T(2,128)S(1)} %pad_maximum_fusion.2), channel_id=1, replica_groups=mesh['tm'=8,'space'=64] {'space'}, use_global_device_ids=true, to_apply=%region_4.6 | all-reduce | flops 512 | bytes 4096 | tf_op jit(solution)/shard_map/psum | solution.py:55
  143.0 33.0 %all-reduce.2.cloned.1.call-done = f32[2,256,256]{2,1,0:T(8,128)} async-done(((f32[2,256,256]{2,1,0:T(8,128)}), f32[2,256,256]{2,1,0:T(8,128)}) %all-reduce.2.cloned.1.call-update) | async-done | bytes 524304 | tf_op jit(solution)/shard_map/psum | solution.py:55
  176.1 1.8 multiply_reduce_fusion.1
  178.6 1.3 select_subtract_fusion.11
  193.1 0.7 select_subtract_fusion
  195.0 0.5 fusion.22
  195.8 6.8 %collective-permute-start = (f32[256,256]{1,0:T(8,128)S(1)}, f32[256,256]{1,0:T(8,128)S(1)}, u32[]{:S(2)}, u32[]{:S(2)}) collective-permute-start(f32[256,256]{1,0:T(8,128)S(1)} %fusion.19), channel_id=1, source_target_pairs={{64,0},{128,64},{192,128},{256,192},{320,256},{384,320},{448,384},... | collective-permute-start | bytes 786440 | tf_op jit(solution)/shard_map/ppermute | solution.py:15
  202.6 5.1 %collective-permute-done = f32[256,256]{1,0:T(8,128)S(1)} collective-permute-done((f32[256,256]{1,0:T(8,128)S(1)}, f32[256,256]{1,0:T(8,128)S(1)}, u32[]{:S(2)}, u32[]{:S(2)}) %collective-permute-start) | collective-permute-done | bytes 262176 | tf_op jit(solution)/shard_map/ppermute | solution.py:15
  208.1 1.9 collective-permute-start.1
  210.1 5.8 %collective-permute-done.1 = f32[256,256]{1,0:T(8,128)S(1)} collective-permute-done((f32[256,256]{1,0:T(8,128)S(1)}, f32[256,256]{1,0:T(8,128)S(1)}, u32[]{:S(2)}, u32[]{:S(2)}) %collective-permute-start.1) | collective-permute-done | bytes 262176 | tf_op jit(solution)/shard_map/ppermute | solution.py:15
  216.2 1.9 collective-permute-start.2
  218.2 5.8 %collective-permute-done.2 = f32[256,256]{1,0:T(8,128)S(1)} collective-permute-done((f32[256,256]{1,0:T(8,128)S(1)}, f32[256,256]{1,0:T(8,128)S(1)}, u32[]{:S(2)}, u32[]{:S(2)}) %collective-permute-start.2) | collective-permute-done | bytes 262176 | tf_op jit(solution)/shard_map/ppermute | solution.py:15
  224.3 1.9 collective-permute-start.3
  226.3 5.8 %collective-permute-done.3 = f32[256,256]{1,0:T(8,128)S(1)} collective-permute-done((f32[256,256]{1,0:T(8,128)S(1)}, f32[256,256]{1,0:T(8,128)S(1)}, u32[]{:S(2)}, u32[]{:S(2)}) %collective-permute-start.3) | collective-permute-done | bytes 262176 | tf_op jit(solution)/shard_map/ppermute | solution.py:15
  232.4 2.1 collective-permute-start.4
  234.5 5.8 %collective-permute-done.4 = f32[256,256]{1,0:T(8,128)S(1)} collective-permute-done((f32[256,256]{1,0:T(8,128)S(1)}, f32[256,256]{1,0:T(8,128)S(1)}, u32[]{:S(2)}, u32[]{:S(2)}) %collective-permute-start.4) | collective-permute-done | bytes 262176 | tf_op jit(solution)/shard_map/ppermute | solution.py:15
  240.7 1.9 collective-permute-start.5
  242.6 5.8 %collective-permute-done.5 = f32[256,256]{1,0:T(8,128)S(1)} collective-permute-done((f32[256,256]{1,0:T(8,128)S(1)}, f32[256,256]{1,0:T(8,128)S(1)}, u32[]{:S(2)}, u32[]{:S(2)}) %collective-permute-start.5) | collective-permute-done | bytes 262176 | tf_op jit(solution)/shard_map/ppermute | solution.py:15
  248.8 1.9 collective-permute-start.6
  250.7 5.8 %collective-permute-done.6 = f32[256,256]{1,0:T(8,128)S(1)} collective-permute-done((f32[256,256]{1,0:T(8,128)S(1)}, f32[256,256]{1,0:T(8,128)S(1)}, u32[]{:S(2)}, u32[]{:S(2)}) %collective-permute-start.6) | collective-permute-done | bytes 262176 | tf_op jit(solution)/shard_map/ppermute | solution.py:15
  257.3 0.5 fusion.1
  257.8 0.5 fusion
  258.5 2.5 copy.5
  (70 shorter events, 18.6 us)
Async XLA Ops:
  6.5 169.5 %all-reduce.2.cloned.1.call-start = ((), (), s32[]{:S(2)}) async-start(), calls=%async_computation | async-start | bytes 1048576 | tf_op jit(solution)/shard_map/psum | solution.py:55
  176.1 4.2 %copy-start.1 = (f32[2,256,256]{2,1,0:T(8,128)S(1)}, f32[2,256,256]{2,1,0:T(8,128)}, u32[]{:S(2)}) copy-start(f32[2,256,256]{2,1,0:T(8,128)} %all-reduce.2.cloned.1.call-done) | copy-start | bytes 1572868
  195.8 11.9 %collective-permute-start = (f32[256,256]{1,0:T(8,128)S(1)}, f32[256,256]{1,0:T(8,128)S(1)}, u32[]{:S(2)}, u32[]{:S(2)}) collective-permute-start(f32[256,256]{1,0:T(8,128)S(1)} %fusion.19), channel_id=1, source_target_pairs={{64,0},{128,64},{192,128},{256,192},{320,256},{384,320},{448,384},... | collective-permute-start | bytes 786440 | tf_op jit(solution)/shard_map/ppermute | solution.py:15
  208.1 7.7 %collective-permute-start.1 = (f32[256,256]{1,0:T(8,128)S(1)}, f32[256,256]{1,0:T(8,128)S(1)}, u32[]{:S(2)}, u32[]{:S(2)}) collective-permute-start(f32[256,256]{1,0:T(8,128)S(1)} %fusion.6), channel_id=1, source_target_pairs={{64,0},{128,64},{192,128},{256,192},{320,256},{384,320},{448,384},... | collective-permute-start | bytes 786440 | tf_op jit(solution)/shard_map/ppermute | solution.py:15
  216.2 7.7 %collective-permute-start.2 = (f32[256,256]{1,0:T(8,128)S(1)}, f32[256,256]{1,0:T(8,128)S(1)}, u32[]{:S(2)}, u32[]{:S(2)}) collective-permute-start(f32[256,256]{1,0:T(8,128)S(1)} %fusion.7), channel_id=1, source_target_pairs={{64,0},{128,64},{192,128},{256,192},{320,256},{384,320},{448,384},... | collective-permute-start | bytes 786440 | tf_op jit(solution)/shard_map/ppermute | solution.py:15
  224.3 7.7 %collective-permute-start.3 = (f32[256,256]{1,0:T(8,128)S(1)}, f32[256,256]{1,0:T(8,128)S(1)}, u32[]{:S(2)}, u32[]{:S(2)}) collective-permute-start(f32[256,256]{1,0:T(8,128)S(1)} %fusion.8), channel_id=1, source_target_pairs={{64,0},{128,64},{192,128},{256,192},{320,256},{384,320},{448,384},... | collective-permute-start | bytes 786440 | tf_op jit(solution)/shard_map/ppermute | solution.py:15
  232.4 24.9 %copy-start = (bf16[2,2048,256]{2,1,0:T(8,128)(2,1)S(1)}, bf16[2,2048,256]{2,1,0:T(8,128)(2,1)}, u32[]{:S(2)}) copy-start(bf16[2,2048,256]{2,1,0:T(8,128)(2,1)} %param.6) | copy-start | bytes 6291460
  232.4 7.8 %collective-permute-start.4 = (f32[256,256]{1,0:T(8,128)S(1)}, f32[256,256]{1,0:T(8,128)S(1)}, u32[]{:S(2)}, u32[]{:S(2)}) collective-permute-start(f32[256,256]{1,0:T(8,128)S(1)} %fusion.9), channel_id=1, source_target_pairs={{64,0},{128,64},{192,128},{256,192},{320,256},{384,320},{448,384},... | collective-permute-start | bytes 786440 | tf_op jit(solution)/shard_map/ppermute | solution.py:15
  240.7 7.7 %collective-permute-start.5 = (f32[256,256]{1,0:T(8,128)S(1)}, f32[256,256]{1,0:T(8,128)S(1)}, u32[]{:S(2)}, u32[]{:S(2)}) collective-permute-start(f32[256,256]{1,0:T(8,128)S(1)} %fusion.10), channel_id=1, source_target_pairs={{64,0},{128,64},{192,128},{256,192},{320,256},{384,320},{448,384},... | collective-permute-start | bytes 786440 | tf_op jit(solution)/shard_map/ppermute | solution.py:15
  248.8 7.7 %collective-permute-start.6 = (f32[256,256]{1,0:T(8,128)S(1)}, f32[256,256]{1,0:T(8,128)S(1)}, u32[]{:S(2)}, u32[]{:S(2)}) collective-permute-start(f32[256,256]{1,0:T(8,128)S(1)} %fusion.11), channel_id=1, source_target_pairs={{64,0},{128,64},{192,128},{256,192},{320,256},{384,320},{448,384},... | collective-permute-start | bytes 786440 | tf_op jit(solution)/shard_map/ppermute | solution.py:15
Sparse Core Ops, SparseCore 0:
  18.7 157.2 all-reduce.1
where the time goes:
time: 268 us
  blocking collectives  123 us (46%)
  waiting for transfers between devices  72.7 us (27%)
  matrix products  23.7 us (9%)
  starting transfers between devices  18.4 us (7%)
  between operations  15.5 us (6%)
  local copies, waits for them, and re-layouts  9.63 us (4%)
  other arithmetic  4.46 us (2%)
    psum x1, blocking collectives, on_device(): gram_all, proj_all = lax.psum((jnp.stack(grams), jnp.stack(projs)), 'space')  123 us
    ppermute x7, waiting for transfers between devices, passed_along(): return lax.ppermute(array, axis, pairs)  39.7 us
    psum x1, waiting for transfers between devices, on_device(): gram_all, proj_all = lax.psum((jnp.stack(grams), jnp.stack(projs)), 'space')  33 us
    ppermute x7, starting transfers between devices, passed_along(): return lax.ppermute(array, axis, pairs)  18.4 us
    dot_general x12, matrix products, finish_transform(): tmat = 1.5 * eye - 0.5 * jnp.dot(zcur, ycur, precision=HIGH)  5.73 us
  transfers between devices with their start and end apart: 8, of which 8 were waited for; matrix products, arithmetic and copies ran while one was open for 0% of the time, Pallas kernels for 0%

commit v1 on v0

v1 whole, which is shorter than its diff:
```python
import jax
import jax.numpy as jnp
from jax import lax
from jax.experimental import pallas as pl
from jax.experimental.pallas import tpu as pltpu
from jax.sharding import PartitionSpec as P

NS_ITERS = 6
M = 256
MESH = pl.DeviceIdType.MESH
F32 = jnp.float32
BF16 = jnp.bfloat16
ORDER = (4, 3, 5, 2, 6, 1, 7)
SHARD = 32
SENT = 40
VMEM_LIMIT = 40 * 2**20


def dot(a, b):
    return jnp.dot(a, b, preferred_element_type=F32)


def dot_nt(a, b):
    return lax.dot_general(a, b, (((1,), (1,)), ((), ())), preferred_element_type=F32)


def dot_tn(a, b):
    return lax.dot_general(a, b, (((0,), (0,)), ((), ())), preferred_element_type=F32)


def split(a):
    high = a.astype(BF16)
    return high, (a - high.astype(F32)).astype(BF16)


def dot3(a, b):
    left = jnp.concatenate([a[0], a[1], a[0]], axis=1)
    right = jnp.concatenate([b[0], b[0], b[1]], axis=0)
    return dot(left, right)


def local_sums(ens, index, value, var):
    inv = 1.0 / var
    low = index & 127
    high = index >> 7
    count = index.shape[1]
    at_low = jnp.where(lax.broadcasted_iota(jnp.int32, (128, count), 0) == low, 1.0, 0.0).astype(BF16)
    at_high = lax.broadcasted_iota(jnp.int32, (16, count), 0) == high
    terms = jnp.concatenate([jnp.where(at_high, inv, 0.0), jnp.where(at_high, value * inv, 0.0)], axis=0)
    first = terms.astype(BF16)
    rest = terms - first.astype(F32)
    second = rest.astype(BF16)
    third = (rest - second.astype(F32)).astype(BF16)
    columns = dot_nt(at_low, first) + (dot_nt(at_low, second) + dot_nt(at_low, third))
    rows = dot_nt(first, at_low) + (dot_nt(second, at_low) + dot_nt(third, at_low))
    s_row = jnp.concatenate([rows[16 + i : 17 + i, :] for i in range(16)], axis=1)
    s_first, s_second = split(s_row)
    s_both = jnp.concatenate([s_first, s_second, jnp.zeros((14, s_row.shape[1]), BF16)], axis=0)
    scaled = [split(ens[128 * i : 128 * (i + 1), :].astype(F32) * columns[:, i : i + 1]) for i in range(16)]
    scaled_first = jnp.concatenate([a for a, _ in scaled], axis=0)
    scaled_second = jnp.concatenate([b for _, b in scaled], axis=0)
    gram = dot_tn(ens, scaled_first) + dot_tn(ens, scaled_second)
    proj = dot(s_both, ens)
    return gram, proj[0:1, :] + proj[1:2, :]


def pack(gram, proj):
    r = lax.broadcasted_iota(jnp.int32, (128, 128), 0)
    c = lax.broadcasted_iota(jnp.int32, (128, 128), 1)
    k11, k12, k22 = gram[:128, :128], gram[:128, 128:], gram[128:, 128:]
    mixed = jnp.where(r >= c, k11, k22)
    diag = jnp.sum(jnp.where(r == c, k22, 0.0), axis=0, keepdims=True)
    extra = jnp.concatenate([diag, proj[:, :128], proj[:, 128:], jnp.zeros((5, 128), F32)], axis=0)
    return jnp.concatenate([k12, mixed], axis=0), extra


def unpack(body, extra):
    r = lax.broadcasted_iota(jnp.int32, (128, 128), 0)
    c = lax.broadcasted_iota(jnp.int32, (128, 128), 1)
    k12, mixed = body[:128, :], body[128:, :]
    turned = mixed.T
    k11 = jnp.where(r >= c, mixed, turned)
    k22 = jnp.where(r < c, mixed, jnp.where(r == c, extra[0:1, :], turned))
    gram = jnp.concatenate(
        [jnp.concatenate([k11, k12], axis=1), jnp.concatenate([k12.T, k22], axis=1)], axis=0
    )
    return gram, jnp.concatenate([extra[1:2, :], extra[2:3, :]], axis=1)


def transforms(sums):
    r = lax.broadcasted_iota(jnp.int32, (M, M), 0)
    c = lax.broadcasted_iota(jnp.int32, (M, M), 1)
    eye = jnp.where(r == c, 1.0, 0.0).astype(F32)
    count = range(len(sums))
    scales, projs, y, z = [], [], [], []
    for gram, proj in sums:
        col_mean = jnp.mean(gram, axis=0, keepdims=True)
        row_mean = jnp.mean(gram, axis=1, keepdims=True)
        amat = gram - row_mean - (col_mean - jnp.mean(col_mean, axis=1, keepdims=True)) + (M - 1.0) * eye
        scale = jnp.sqrt(jnp.sum(jnp.sum(amat * amat, axis=0, keepdims=True), axis=1, keepdims=True))
        start = amat / scale
        proj = proj - col_mean
        projs.append(proj - jnp.mean(proj, axis=1, keepdims=True))
        scales.append(scale)
        y.append(split(start))
        z.append(split(1.5 * eye - 0.5 * start))
    y = [split(dot3(y[w], z[w])) for w in count]
    for step in range(1, NS_ITERS):
        t = [split(1.5 * eye - 0.5 * dot3(z[w], y[w])) for w in count]
        last = [dot3(t[w], z[w]) for w in count]
        z = [split(last[w]) for w in count]
        if step < NS_ITERS - 1:
            y = [split(dot3(y[w], t[w])) for w in count]
    gmats = []
    for w in count:
        vec = dot3(split(jnp.broadcast_to(projs[w], (16, M))), z[w])
        vec = split(vec)
        mean = dot_nt(z[w][0], vec[0]) + (dot_nt(z[w][0], vec[1]) + dot_nt(z[w][1], vec[0]))
        wmean = mean[:, 0:1] / scales[w]
        wmean = wmean - jnp.mean(wmean, axis=0, keepdims=True)
        wtrans = last[w] * (jnp.sqrt(M - 1.0) / jnp.sqrt(scales[w]))
        gmats.append(wmean + (wtrans - jnp.mean(wtrans, axis=0, keepdims=True) + 1.0 / M))
    return gmats


def suffix_kernel(
    ens_ref, index_ref, value_ref, var_ref, out_ref,
    parts, got1, mine, got2, whole, extras, pair, half, chips, later,
    send1, recv1, send2, recv2, send3, recv3, core_send, core_recv, x_send, x_recv, f_send, f_recv,
):
    t = lax.axis_index("tm")
    s = lax.axis_index("space")
    x, core = t // 2, t % 2
    at = (s // 8, s % 8)

    def along(axis, by):
        spot = list(at)
        spot[axis] = (at[axis] + by) % 8
        return {"tm": t, "space": spot[0] * 8 + spot[1]}

    def on_x(by):
        return {"tm": ((x + by + 4) % 4) * 2 + core, "space": s}

    sibling = {"tm": x * 2 + 1 - core, "space": s}

    barrier = pltpu.get_barrier_semaphore()
    for by in ORDER:
        for axis in range(2):
            pl.semaphore_signal(barrier, inc=1, device_id=along(axis, by), device_id_type=MESH)
    for by in (1, 2, 3):
        pl.semaphore_signal(barrier, inc=1, device_id=on_x(by), device_id_type=MESH)
    pl.semaphore_signal(barrier, inc=1, device_id=sibling, device_id_type=MESH)

    def copy1(w, i):
        by = ORDER[i]
        return pltpu.make_async_remote_copy(
            src_ref=parts.at[w, (at[w] + by) % 8], dst_ref=got1.at[w, i], send_sem=send1.at[w, i],
            recv_sem=recv1.at[w, i], device_id=along(w, by), device_id_type=MESH,
        )

    def copy2(w, i):
        return pltpu.make_async_remote_copy(
            src_ref=mine.at[w], dst_ref=got2.at[w, i], send_sem=send2.at[w, i],
            recv_sem=recv2.at[w, i], device_id=along(1 - w, ORDER[i]), device_id_type=MESH,
        )

    def copy3(w, i):
        return pltpu.make_async_remote_copy(
            src_ref=whole.at[w, at[w]], dst_ref=whole.at[w, at[w]], send_sem=send3.at[w, i],
            recv_sem=recv3.at[w, i], device_id=along(w, ORDER[i]), device_id_type=MESH,
        )

    for w in range(2):
        gram, proj = local_sums(ens_ref[w], index_ref[w : w + 1, :], value_ref[w : w + 1, :], var_ref[w : w + 1, :])
        body, extra = pack(gram, proj)
        for k in range(8):
            parts[w, k, 0:SHARD, :] = body[SHARD * k : SHARD * (k + 1), :]
            parts[w, k, SHARD:SENT, :] = extra
        if w == 0:
            pl.semaphore_wait(barrier, 18)
        for i in range(7):
            copy1(w, i).start()

    for w in range(2):
        total = parts[w, at[w]]
        for i in range(7):
            copy1(w, i).wait_recv()
            total = total + got1[w, i]
        mine[w] = total
        for i in range(7):
            copy2(w, i).start()

    for w in range(2):
        total = mine[w]
        for i in range(7):
            copy2(w, i).wait_recv()
            total = total + got2[w, i]
        whole[w, at[w]] = total[:SHARD]
        extras[w] = total[SHARD:]
        for i in range(7):
            copy3(w, i).start()

    for w in range(2):
        for i in range(7):
            copy1(w, i).wait_send()
            copy2(w, i).wait_send()
    for w in range(2):
        for i in range(7):
            copy3(w, i).wait_recv()

    g0, g1 = transforms([unpack(whole[w].reshape(256, 128), extras[w]) for w in range(2)])
    g0, g1 = split(g0), split(g1)
    own = dot3(g0, g1)
    pair[core] = own
    swap = pltpu.make_async_remote_copy(
        src_ref=pair.at[core], dst_ref=pair.at[core], send_sem=core_send, recv_sem=core_recv,
        device_id=sibling, device_id_type=MESH,
    )
    swap.start()
    r = lax.broadcasted_iota(jnp.int32, (128, M), 0)
    c = lax.broadcasted_iota(jnp.int32, (128, M), 1)
    for j in range(3):
        @pl.when(j < x)
        def _():
            for h in range(2):
                chips[j, h] = jnp.where(r + 128 * h == c, 1.0, 0.0).astype(F32)
    swap.wait()
    odd = split(pair[1])
    half[...] = dot3(split(pair[0, pl.ds(pl.multiple_of(core * 128, 128), 128), :]), odd)

    def copy_x(by):
        return pltpu.make_async_remote_copy(
            src_ref=half, dst_ref=chips.at[x - 1, core], send_sem=x_send.at[by - 1], recv_sem=x_recv.at[x - 1],
            device_id=on_x(-by), device_id_type=MESH,
        )

    def arrived(j):
        return pltpu.make_async_remote_copy(
            src_ref=half, dst_ref=chips.at[j, core], send_sem=x_send.at[0], recv_sem=x_recv.at[j],
            device_id=sibling, device_id_type=MESH,
        )

    def pass_on(j):
        return pltpu.make_async_remote_copy(
            src_ref=chips.at[j, core], dst_ref=chips.at[j, core], send_sem=f_send.at[j], recv_sem=f_recv.at[j],
            device_id=sibling, device_id_type=MESH,
        )

    def passed(j):
        return pltpu.make_async_remote_copy(
            src_ref=chips.at[j, core], dst_ref=chips.at[j, 1 - core], send_sem=f_send.at[j], recv_sem=f_recv.at[j],
            device_id=sibling, device_id_type=MESH,
        )

    for by in (1, 2, 3):
        @pl.when(x >= by)
        def _():
            copy_x(by).start()
    for j in range(3):
        @pl.when(x <= j)
        def _():
            arrived(j).wait_recv()
            pass_on(j).start()
    for j in range(3):
        @pl.when(x <= j)
        def _():
            passed(j).wait_recv()
    for w in range(2):
        for i in range(7):
            copy3(w, i).wait_send()
    second = split(dot3(split(chips[1].reshape(M, M)), split(chips[2].reshape(M, M))))
    after = dot3(split(chips[0].reshape(M, M)), second)
    later[...] = after

    @pl.when(core == 0)
    def _():
        later[...] = dot3(odd, split(after))

    tail = split(later[...])
    out_ref[1] = dot3(g1, tail).astype(BF16)
    out_ref[0] = dot3(split(own), tail).astype(BF16)
    for by in (1, 2, 3):
        @pl.when(x >= by)
        def _():
            copy_x(by).wait_send()
    for j in range(3):
        @pl.when(x <= j)
        def _():
            pass_on(j).wait_send()


def smooth_kernel(ens_ref, suffix_ref, out_ref, held, sem):
    steps = held.shape[0]
    rows = held.shape[1]
    each = steps // 2

    def copy(i):
        return pltpu.make_async_copy(held.at[i], out_ref.at[i // each, pl.ds((i % each) * rows, rows)], sem.at[i])

    for i in range(steps):
        block = ens_ref[i // each, (i % each) * rows : (i % each + 1) * rows, :]
        held[i] = dot(block, suffix_ref[i // each]).astype(BF16)
        copy(i).start()
    for i in range(steps):
        copy(i).wait()


def on_device(ensemble, obs_index, obs_value, obs_var):
    vmem = pl.BlockSpec(memory_space=pltpu.VMEM)
    sems = pltpu.SemaphoreType.DMA
    suffix = pl.pallas_call(
        suffix_kernel,
        out_shape=jax.ShapeDtypeStruct((2, M, M), BF16),
        in_specs=[vmem] * 4,
        out_specs=vmem,
        scratch_shapes=[
            pltpu.VMEM((2, 8, SENT, 128), F32),
            pltpu.VMEM((2, 7, SENT, 128), F32),
            pltpu.VMEM((2, SENT, 128), F32),
            pltpu.VMEM((2, 7, SENT, 128), F32),
            pltpu.VMEM((2, 8, SHARD, 128), F32),
            pltpu.VMEM((2, 8, 128), F32),
            pltpu.VMEM((2, M, M), F32),
            pltpu.VMEM((128, M), F32),
            pltpu.VMEM((3, 2, 128, M), F32),
            pltpu.VMEM((M, M), F32),
            sems((2, 7)), sems((2, 7)), sems((2, 7)), sems((2, 7)), sems((2, 7)), sems((2, 7)),
            sems, sems, sems((3,)), sems((3,)), sems((3,)), sems((3,)),
        ],
        compiler_params=pltpu.CompilerParams(collective_id=0, has_side_effects=True, vmem_limit_bytes=VMEM_LIMIT),
        name="suffixes",
    )(ensemble, obs_index, obs_value, obs_var)
    return pl.pallas_call(
        smooth_kernel,
        out_shape=jax.ShapeDtypeStruct(ensemble.shape, BF16),
        in_specs=[vmem] * 2,
        out_specs=pl.BlockSpec(memory_space=pltpu.HBM),
        scratch_shapes=[pltpu.VMEM((8, ensemble.shape[1] // 4, M), BF16), sems((8,))],
        compiler_params=pltpu.CompilerParams(vmem_limit_bytes=VMEM_LIMIT),
        name="smooth",
    )(ensemble, suffix)


def solution(mesh):
    placed = (P("tm", "space", None), P("tm", "space"), P("tm", "space"), P("tm", "space"))
    return jax.shard_map(
        on_device, mesh=mesh, in_specs=placed, out_specs=P("tm", "space", None), check_vma=False
    )
```

time: 268 us -> 59.1 us (0.22)
  blocking collectives: 123 us -> 0 us
  waiting for transfers between devices: 72.7 us -> 0 us
  Pallas kernels: 0 us -> 55.2 us
  matrix products: 23.7 us -> 0 us
  starting transfers between devices: 18.4 us -> 0 us
  between operations: 15.5 us -> 0.01 us
  local copies, waits for them, and re-layouts: 9.63 us -> 3.65 us
  other arithmetic: 4.46 us -> 0 us
    psum x1 -> x0, blocking collectives: 123 us -> none  [on_device(): gram_all, proj_all = lax.psum((jnp.stack(grams), jnp.stack(projs)), 'space')]
    pallas_call x0 -> x2, Pallas kernels: none -> 55.2 us  [the longest x1 53.5 us: on_device(): pl.pallas_call(suffix_kernel, out_shape=jax.ShapeDtypeStruct((2, M, M), B...]
    ppermute x7 -> x0, waiting for transfers between devices: 39.7 us -> none  [passed_along(): return lax.ppermute(array, axis, pairs)]
    psum x1 -> x0, waiting for transfers between devices: 33 us -> none  [on_device(): gram_all, proj_all = lax.psum((jnp.stack(grams), jnp.stack(projs)), 'space')]
    dot_general x54 -> x0, matrix products: 23.7 us -> none  [the longest x12 5.73 us: finish_transform(): tmat = 1.5 * eye - 0.5 * jnp.dot(zcur, ycur, precision=HIGH)]
    ppermute x7 -> x0, starting transfers between devices: 18.4 us -> none  [passed_along(): return lax.ppermute(array, axis, pairs)]
    gather x2 -> x0, local copies, waits for them, and re-layouts: 3.91 us -> none  [on_device(): rows = jnp.take(ensemble[w], obs_index[w], axis=0).astype(jnp.float32)]
    unnamed x4 -> x8, local copies, waits for them, and re-layouts: 0.01 us -> 3.65 us
  transfers between devices with their start and end apart: 8 -> 0, of which waited for: 8 -> 0; matrix products, arithmetic and copies ran while one was open for 0% -> 0% of each run, Pallas kernels for 0% -> 0%
where the time goes in v1:
time: 59.1 us; the launch traced here: 58.8 us
  Pallas kernels  55.2 us (93%)
  local copies, waits for them, and re-layouts  3.65 us (6%)
    pallas_call x1, Pallas kernels, on_device(): pl.pallas_call(suffix_kernel, out_shape=jax.ShapeDtypeStruct((2, M, M), B...  53.5 us
    unnamed x8, local copies, waits for them, and re-layouts  3.65 us
    pallas_call x1, Pallas kernels, on_device(): pl.pallas_call(smooth_kernel, out_shape=jax.ShapeDtypeStruct(ensemble.sha...  1.68 us

profile of v1, /device:TPU:1, one launch (start us, length us, event | category | flops | bytes accessed | tf_op | source)
XLA Modules:
  0.0 58.8 jit_solution(11079131791144422714)
XLA Ops:
  0.0 0.0 copy-start
  0.0 1.6 %copy-done = bf16[2,2048,256]{2,1,0:T(8,128)(2,1)S(1)} copy-done((bf16[2,2048,256]{2,1,0:T(8,128)(2,1)S(1)}, bf16[2,2048,256]{2,1,0:T(8,128)(2,1)}, u32[]{:S(2)}) %copy-start) | copy-done | bytes 2097176
  1.6 0.0 copy-start.1
  1.6 0.7 %copy-done.1 = s32[2,512]{1,0:T(2,128)S(1)} copy-done((s32[2,512]{1,0:T(2,128)S(1)}, s32[2,512]{1,0:T(2,128)}, u32[]{:S(2)}) %copy-start.1) | copy-done | bytes 4120
  2.3 0.0 copy-start.2
  2.3 0.7 %copy-done.2 = f32[2,512]{1,0:T(2,128)S(1)} copy-done((f32[2,512]{1,0:T(2,128)S(1)}, f32[2,512]{1,0:T(2,128)}, u32[]{:S(2)}) %copy-start.2) | copy-done | bytes 4120
  3.0 0.0 copy-start.3
  3.0 0.7 %copy-done.3 = f32[2,512]{1,0:T(2,128)S(1)} copy-done((f32[2,512]{1,0:T(2,128)S(1)}, f32[2,512]{1,0:T(2,128)}, u32[]{:S(2)}) %copy-start.3) | copy-done | bytes 4120
  3.7 53.5 %suffixes.1.suffix_ref = bf16[2,256,256]{2,1,0:T(8,128)(2,1)S(1)} custom-call(bf16[2,2048,256]{2,1,0:T(8,128)(2,1)S(1)} %copy-done, s32[2,512]{1,0:T(2,128)S(1)} %copy-done.1, f32[2,512]{1,0:T(2,128)S(1)} %copy-done.2, f32[2,512]{1,0:T(2,128)S(1)} %copy-done.3), custom_call_target="tpu_custom_call" | custom-call | tf_op jit(solution)/shard_map/suffixes/pallas_call | solution.py:311
  57.2 1.7 %smooth.1 = bf16[2,2048,256]{2,1,0:T(8,128)(2,1)} custom-call(bf16[2,2048,256]{2,1,0:T(8,128)(2,1)S(1)} %copy-done, bf16[2,256,256]{2,1,0:T(8,128)(2,1)S(1)} %suffixes.1.suffix_ref), custom_call_target="tpu_custom_call" | custom-call | tf_op jit(solution)/shard_map/smooth/pallas_call | solution.py:333
Async XLA Ops:
  0.0 1.6 %copy-start = (bf16[2,2048,256]{2,1,0:T(8,128)(2,1)S(1)}, bf16[2,2048,256]{2,1,0:T(8,128)(2,1)}, u32[]{:S(2)}) copy-start(bf16[2,2048,256]{2,1,0:T(8,128)(2,1)} %ens_ref.3) | copy-start | bytes 6291460
  1.6 0.7 %copy-start.1 = (s32[2,512]{1,0:T(2,128)S(1)}, s32[2,512]{1,0:T(2,128)}, u32[]{:S(2)}) copy-start(s32[2,512]{1,0:T(2,128)} %index_ref.1) | copy-start | bytes 12292
  2.3 0.7 %copy-start.2 = (f32[2,512]{1,0:T(2,128)S(1)}, f32[2,512]{1,0:T(2,128)}, u32[]{:S(2)}) copy-start(f32[2,512]{1,0:T(2,128)} %value_ref.1) | copy-start | bytes 12292
  3.0 0.7 %copy-start.3 = (f32[2,512]{1,0:T(2,128)S(1)}, f32[2,512]{1,0:T(2,128)}, u32[]{:S(2)}) copy-start(f32[2,512]{1,0:T(2,128)} %var_ref.1) | copy-start | bytes 12292

commit v2 on v1

--- a/solution.py
+++ b/solution.py
@@ -13,7 +13,7 @@
 ORDER = (4, 3, 5, 2, 6, 1, 7)
 SHARD = 32
 SENT = 40
-VMEM_LIMIT = 40 * 2**20
+VMEM_LIMIT = 20 * 2**20
 
 
 def dot(a, b):
@@ -124,8 +124,8 @@
 
 
 def suffix_kernel(
-    ens_ref, index_ref, value_ref, var_ref, out_ref,
-    parts, got1, mine, got2, whole, extras, pair, half, chips, later,
+    ens_in, index_in, value_in, var_in, out_ref, ens_ref,
+    index_ref, value_ref, var_ref, load, parts, got1, mine, got2, whole, extras, pair, half, chips, later,
     send1, recv1, send2, recv2, send3, recv3, core_send, core_recv, x_send, x_recv, f_send, f_recv,
 ):
     t = lax.axis_index("tm")
@@ -142,6 +142,12 @@
         return {"tm": ((x + by + 4) % 4) * 2 + core, "space": s}
 
     sibling = {"tm": x * 2 + 1 - core, "space": s}
+
+    pairs = ((index_in, index_ref), (value_in, value_ref), (var_in, var_ref))
+    loads = [pltpu.make_async_copy(a, b, load.at[i]) for i, (a, b) in enumerate(pairs)]
+    loads += [pltpu.make_async_copy(ens_in.at[w], ens_ref.at[w], load.at[3 + w]) for w in range(2)]
+    for copy in loads:
+        copy.start()
 
     barrier = pltpu.get_barrier_semaphore()
     for by in ORDER:
@@ -170,7 +176,10 @@
             recv_sem=recv3.at[w, i], device_id=along(w, ORDER[i]), device_id_type=MESH,
         )
 
-    for w in range(2):
+    for copy in loads[:3]:
+        copy.wait()
+    for w in range(2):
+        loads[3 + w].wait()
         gram, proj = local_sums(ens_ref[w], index_ref[w : w + 1, :], value_ref[w : w + 1, :], var_ref[w : w + 1, :])
         body, extra = pack(gram, proj)
         for k in range(8):
@@ -308,12 +317,14 @@
 def on_device(ensemble, obs_index, obs_value, obs_var):
     vmem = pl.BlockSpec(memory_space=pltpu.VMEM)
     sems = pltpu.SemaphoreType.DMA
-    suffix = pl.pallas_call(
+    small = [pltpu.VMEM(a.shape, a.dtype) for a in (obs_index, obs_value, obs_var)]
+    suffix, held = pl.pallas_call(
         suffix_kernel,
-        out_shape=jax.ShapeDtypeStruct((2, M, M), BF16),
-        in_specs=[vmem] * 4,
-        out_specs=vmem,
-        scratch_shapes=[
+        out_shape=(jax.ShapeDtypeStruct((2, M, M), BF16), jax.ShapeDtypeStruct(ensemble.shape, BF16)),
+        in_specs=[pl.BlockSpec(memory_space=pltpu.HBM)] * 4,
+        out_specs=(vmem, vmem),
+        scratch_shapes=small + [
+            sems((5,)),
             pltpu.VMEM((2, 8, SENT, 128), F32),
             pltpu.VMEM((2, 7, SENT, 128), F32),
             pltpu.VMEM((2, SENT, 128), F32),
@@ -329,7 +340,7 @@
         ],
         compiler_params=pltpu.CompilerParams(collective_id=0, has_side_effects=True, vmem_limit_bytes=VMEM_LIMIT),
         name="suffixes",
-    )(ensemble, obs_index, obs_value, obs_var)
+    )(*(pltpu.with_memory_space_constraint(a, pltpu.HBM) for a in (ensemble, obs_index, obs_value, obs_var)))
     return pl.pallas_call(
         smooth_kernel,
         out_shape=jax.ShapeDtypeStruct(ensemble.shape, BF16),
@@ -338,7 +349,7 @@
         scratch_shapes=[pltpu.VMEM((8, ensemble.shape[1] // 4, M), BF16), sems((8,))],
         compiler_params=pltpu.CompilerParams(vmem_limit_bytes=VMEM_LIMIT),
         name="smooth",
-    )(ensemble, suffix)
+    )(held, suffix)
 
 
 def solution(mesh):

time: 59.1 us -> 55.1 us (0.932)
  local copies, waits for them, and re-layouts: 3.65 us -> 0 us
    unnamed x8 -> x0, local copies, waits for them, and re-layouts: 3.65 us -> none
where the time goes in v2:
time: 55.1 us; the launch traced here: 55 us
  Pallas kernels  55 us (100%)
    pallas_call x1, Pallas kernels, on_device(): pl.pallas_call(suffix_kernel, out_shape=(jax.ShapeDtypeStruct((2, M, M),...  53.3 us
    pallas_call x1, Pallas kernels, on_device(): pl.pallas_call(smooth_kernel, out_shape=jax.ShapeDtypeStruct(ensemble.sha...  1.68 us

profile of v2, /device:TPU:1, one launch (start us, length us, event | category | flops | bytes accessed | tf_op | source)
XLA Modules:
  0.0 55.0 jit_solution(13438510467832584578)
XLA Ops:
  0.0 53.3 %suffixes.1 = (bf16[2,256,256]{2,1,0:T(8,128)(2,1)S(1)}, bf16[2,2048,256]{2,1,0:T(8,128)(2,1)S(1)}) custom-call(bf16[2,2048,256]{2,1,0:T(8,128)(2,1)} %ens_in.1, s32[2,512]{1,0:T(2,128)} %index_in.1, f32[2,512]{1,0:T(2,128)} %value_in.1, f32[2,512]{1,0:T(2,128)} %var_in.1), custom_call_target="tpu_custom_call" | custom-call | tf_op jit(solution)/shard_map/suffixes/pallas_call | solution.py:321
  53.3 1.7 %smooth.1 = bf16[2,2048,256]{2,1,0:T(8,128)(2,1)} custom-call(bf16[2,2048,256]{2,1,0:T(8,128)(2,1)S(1)} %get-tuple-element.7.ens_ref, bf16[2,256,256]{2,1,0:T(8,128)(2,1)S(1)} %get-tuple-element.8.suffix_ref), custom_call_target="tpu_custom_call" | custom-call | tf_op jit(solution)/shard_map/smooth/pallas_call | solution.py:344

commit v3 on v2

v3 whole, which is shorter than its diff:
```python
import jax
import jax.numpy as jnp
from jax import lax
from jax.experimental import pallas as pl
from jax.experimental.pallas import tpu as pltpu
from jax.sharding import PartitionSpec as P

NS_ITERS = 6
M = 256
MESH = pl.DeviceIdType.MESH
F32 = jnp.float32
BF16 = jnp.bfloat16
ORDER = (4, 3, 5, 2, 6, 1, 7)
SHARD = 16
CHUNK = 64
VMEM_LIMIT = 20 * 2**20


def dot(a, b):
    return jnp.dot(a, b, preferred_element_type=F32)


def dot_nt(a, b):
    return lax.dot_general(a, b, (((1,), (1,)), ((), ())), preferred_element_type=F32)


def dot_tn(a, b):
    return lax.dot_general(a, b, (((0,), (0,)), ((), ())), preferred_element_type=F32)


def split(a):
    high = a.astype(BF16)
    return high, (a - high.astype(F32)).astype(BF16)


def dot3(a, b):
    left = jnp.concatenate([a[0], a[1], a[0]], axis=1)
    right = jnp.concatenate([b[0], b[0], b[1]], axis=0)
    return dot(left, right)


def row_sums(index, value, var):
    inv = 1.0 / var
    low = index & 127
    high = index >> 7
    count = index.shape[1]
    at_low = jnp.where(lax.broadcasted_iota(jnp.int32, (128, count), 0) == low, 1.0, 0.0).astype(BF16)
    at_high = lax.broadcasted_iota(jnp.int32, (16, count), 0) == high
    terms = jnp.concatenate([jnp.where(at_high, inv, 0.0), jnp.where(at_high, value * inv, 0.0)], axis=0)
    first = terms.astype(BF16)
    rest = terms - first.astype(F32)
    second = rest.astype(BF16)
    third = (rest - second.astype(F32)).astype(BF16)
    columns = dot_nt(at_low, first) + (dot_nt(at_low, second) + dot_nt(at_low, third))
    rows = dot_nt(first, at_low) + (dot_nt(second, at_low) + dot_nt(third, at_low))
    s_row = jnp.concatenate([rows[16 + i : 17 + i, :] for i in range(16)], axis=1)
    s_first, s_second = split(s_row)
    return columns, jnp.concatenate([s_first, s_second, jnp.zeros((14, s_row.shape[1]), BF16)], axis=0)


def local_sums(ens, columns, s_both):
    scaled = [split(ens[128 * i : 128 * (i + 1), :].astype(F32) * columns[:, i : i + 1]) for i in range(16)]
    scaled_first = jnp.concatenate([a for a, _ in scaled], axis=0)
    scaled_second = jnp.concatenate([b for _, b in scaled], axis=0)
    gram = dot_tn(ens, scaled_first) + dot_tn(ens, scaled_second)
    proj = dot(s_both, ens)
    return gram, proj[0:1, :] + proj[1:2, :]


def pack(gram, proj):
    r = lax.broadcasted_iota(jnp.int32, (128, 128), 0)
    c = lax.broadcasted_iota(jnp.int32, (128, 128), 1)
    k11, k12, k22 = gram[:128, :128], gram[:128, 128:], gram[128:, 128:]
    mixed = jnp.where(r >= c, k11, k22)
    diag = jnp.sum(jnp.where(r == c, k22, 0.0), axis=0, keepdims=True)
    extra = jnp.concatenate([diag, proj[:, :128], proj[:, 128:], jnp.zeros((5, 128), F32)], axis=0)
    return k12, mixed, extra


def unpack(k12, mixed, extra):
    r = lax.broadcasted_iota(jnp.int32, (128, 128), 0)
    c = lax.broadcasted_iota(jnp.int32, (128, 128), 1)
    turned = mixed.T
    k11 = jnp.where(r >= c, mixed, turned)
    k22 = jnp.where(r < c, mixed, jnp.where(r == c, extra[0:1, :], turned))
    gram = jnp.concatenate(
        [jnp.concatenate([k11, k12], axis=1), jnp.concatenate([k12.T, k22], axis=1)], axis=0
    )
    return gram, jnp.concatenate([extra[1:2, :], extra[2:3, :]], axis=1)


def transforms(sums):
    r = lax.broadcasted_iota(jnp.int32, (M, M), 0)
    c = lax.broadcasted_iota(jnp.int32, (M, M), 1)
    eye = jnp.where(r == c, 1.0, 0.0).astype(F32)
    count = range(len(sums))

    def twice(a, b):
        return dot(jnp.concatenate([a, a], axis=1), jnp.concatenate(b, axis=0))

    def after(a, b):
        return dot(jnp.concatenate(a, axis=1), jnp.concatenate([b, b], axis=0))

    scales, projs, y, z = [], [], [], []
    for gram, proj in sums:
        col_mean = jnp.mean(gram, axis=0, keepdims=True)
        row_mean = jnp.mean(gram, axis=1, keepdims=True)
        amat = gram - row_mean - (col_mean - jnp.mean(col_mean, axis=1, keepdims=True)) + (M - 1.0) * eye
        scale = jnp.sqrt(jnp.sum(jnp.sum(amat * amat, axis=0, keepdims=True), axis=1, keepdims=True))
        start = amat * (1.0 / scale)
        proj = proj - col_mean
        projs.append(proj - jnp.mean(proj, axis=1, keepdims=True))
        scales.append(scale)
        b = (0.5 * start).astype(BF16)
        y.append(1.5 * start - after(split(start), b))
        z.append(1.5 * eye - b.astype(F32))
    for step in range(1, NS_ITERS - 1):
        zs, ys = [split(a) for a in z], [split(a) for a in y]
        b = [(0.5 * dot(zs[w][0], ys[w][0])).astype(BF16) for w in count]
        z = [1.5 * z[w] - twice(b[w], zs[w]) for w in count]
        y = [1.5 * y[w] - after(ys[w], b[w]) for w in count]
    zs, ys = [split(a) for a in z], [split(a) for a in y]
    t = [split(1.5 * eye - 0.5 * dot3(zs[w], ys[w])) for w in count]
    z = [dot3(t[w], zs[w]) for w in count]
    turned = []
    for w in count:
        both = split(z[w])
        vec = dot3(split(jnp.broadcast_to(projs[w], (16, M))), both)
        wmean = dot3(split(vec), both)[0:1, :] / scales[w]
        wmean = wmean - jnp.mean(wmean, axis=1, keepdims=True)
        wtrans = z[w] * (jnp.sqrt(M - 1.0) / jnp.sqrt(scales[w]))
        turned.append(wtrans - jnp.mean(wtrans, axis=1, keepdims=True) + (wmean + 1.0 / M))
    return turned


def suffix_kernel(
    ens_in, index_in, value_in, var_in, out_ref, ens_ref,
    index_ref, value_ref, var_ref, load, parts, got1, mine, got2, whole, extras, pair, half, chips, tail,
    send1, recv1, send2, recv2, send3, recv3, core_send, core_recv, x_send, x_recv, f_send, f_recv,
):
    t = lax.axis_index("tm")
    s = lax.axis_index("space")
    x, core = t // 2, t % 2
    at = (s // 8, s % 8)

    def along(axis, by):
        spot = list(at)
        spot[axis] = (at[axis] + by) % 8
        return {"tm": t, "space": spot[0] * 8 + spot[1]}

    def on_x(by):
        return {"tm": ((x + by + 4) % 4) * 2 + core, "space": s}

    sibling = {"tm": x * 2 + 1 - core, "space": s}

    pairs = ((index_in, index_ref), (value_in, value_ref), (var_in, var_ref))
    loads = [pltpu.make_async_copy(a, b, load.at[i]) for i, (a, b) in enumerate(pairs)]
    loads += [pltpu.make_async_copy(ens_in.at[w], ens_ref.at[w], load.at[3 + w]) for w in range(2)]
    for copy in loads:
        copy.start()

    barrier = pltpu.get_barrier_semaphore()
    for by in ORDER:
        for axis in range(2):
            pl.semaphore_signal(barrier, inc=1, device_id=along(axis, by), device_id_type=MESH)
    for by in (1, 2, 3):
        pl.semaphore_signal(barrier, inc=1, device_id=on_x(by), device_id_type=MESH)
    pl.semaphore_signal(barrier, inc=1, device_id=sibling, device_id_type=MESH)

    blocks = [(w, p) for w in range(2) for p in range(2)]

    def axis_of(w, p):
        return (w + p) % 2

    def sent(p):
        return pl.ds(0, SHARD + 8 * p)

    def copy1(w, p, i):
        axis, by = axis_of(w, p), ORDER[i]
        return pltpu.make_async_remote_copy(
            src_ref=parts.at[w, p, (at[axis] + by) % 8, sent(p)], dst_ref=got1.at[w, p, i, sent(p)],
            send_sem=send1.at[w, p, i], recv_sem=recv1.at[w, p, i], device_id=along(axis, by), device_id_type=MESH,
        )

    def copy2(w, p, i):
        return pltpu.make_async_remote_copy(
            src_ref=mine.at[w, p, sent(p)], dst_ref=got2.at[w, p, i, sent(p)],
            send_sem=send2.at[w, p, i], recv_sem=recv2.at[w, p, i],
            device_id=along(1 - axis_of(w, p), ORDER[i]), device_id_type=MESH,
        )

    def copy3(w, p, i):
        axis = axis_of(w, p)
        return pltpu.make_async_remote_copy(
            src_ref=whole.at[w, p, at[axis]], dst_ref=whole.at[w, p, at[axis]],
            send_sem=send3.at[w, p, i], recv_sem=recv3.at[w, p, i], device_id=along(axis, ORDER[i]), device_id_type=MESH,
        )

    for copy in loads[:3]:
        copy.wait()
    sums = [row_sums(index_ref[w : w + 1, :], value_ref[w : w + 1, :], var_ref[w : w + 1, :]) for w in range(2)]
    for w in range(2):
        loads[3 + w].wait()
        k12, mixed, extra = pack(*local_sums(ens_ref[w], *sums[w]))
        for k in range(8):
            parts[w, 0, k, 0:SHARD, :] = k12[SHARD * k : SHARD * (k + 1), :]
            parts[w, 1, k, 0:SHARD, :] = mixed[SHARD * k : SHARD * (k + 1), :]
            parts[w, 1, k, SHARD:, :] = extra
        if w == 0:
            pl.semaphore_wait(barrier, 18)
        for i in range(7):
            for p in range(2):
                copy1(w, p, i).start()

    for w, p in blocks:
        total = parts[w, p, at[axis_of(w, p)], sent(p)]
        for i in range(7):
            copy1(w, p, i).wait_recv()
            total = total + got1[w, p, i, sent(p)]
        mine[w, p, sent(p)] = total
        for i in range(7):
            copy2(w, p, i).start()

    for w, p in blocks:
        total = mine[w, p, sent(p)]
        for i in range(7):
            copy2(w, p, i).wait_recv()
            total = total + got2[w, p, i, sent(p)]
        whole[w, p, at[axis_of(w, p)]] = total[:SHARD]
        if p == 1:
            extras[w] = total[SHARD:]
        for i in range(7):
            copy3(w, p, i).start()

    for w, p in blocks:
        for i in range(7):
            copy1(w, p, i).wait_send()
    for w, p in blocks:
        for i in range(7):
            copy3(w, p, i).wait_recv()

    h0, h1 = transforms(
        [unpack(whole[w, 0].reshape(128, 128), whole[w, 1].reshape(128, 128), extras[w]) for w in range(2)]
    )
    h0, h1 = split(h0), split(h1)
    own = dot3(h1, h0)
    pair[core] = own
    swap = pltpu.make_async_remote_copy(
        src_ref=pair.at[core], dst_ref=pair.at[core], send_sem=core_send, recv_sem=core_recv,
        device_id=sibling, device_id_type=MESH,
    )
    swap.start()
    for w, p in blocks:
        for i in range(7):
            copy2(w, p, i).wait_send()
    for w, p in blocks:
        for i in range(7):
            copy3(w, p, i).wait_send()
    swap.wait()
    even = split(pair[0])

    def copy_x(by, n):
        rows = pl.ds(CHUNK * n, CHUNK)
        return pltpu.make_async_remote_copy(
            src_ref=half.at[rows], dst_ref=chips.at[x - 1, core, rows], send_sem=x_send.at[by - 1, n],
            recv_sem=x_recv.at[x - 1, n], device_id=on_x(-by), device_id_type=MESH,
        )

    def arrived(j, n):
        rows = pl.ds(CHUNK * n, CHUNK)
        return pltpu.make_async_remote_copy(
            src_ref=half.at[rows], dst_ref=chips.at[j, core, rows], send_sem=x_send.at[0, n],
            recv_sem=x_recv.at[j, n], device_id=sibling, device_id_type=MESH,
        )

    def pass_on(j, n):
        rows = pl.ds(CHUNK * n, CHUNK)
        return pltpu.make_async_remote_copy(
            src_ref=chips.at[j, core, rows], dst_ref=chips.at[j, core, rows], send_sem=f_send.at[j, n],
            recv_sem=f_recv.at[j, n], device_id=sibling, device_id_type=MESH,
        )

    def passed(j, n):
        rows = pl.ds(CHUNK * n, CHUNK)
        return pltpu.make_async_remote_copy(
            src_ref=chips.at[j, core, rows], dst_ref=chips.at[j, 1 - core, rows], send_sem=f_send.at[j, n],
            recv_sem=f_recv.at[j, n], device_id=sibling, device_id_type=MESH,
        )

    for n in range(128 // CHUNK):
        top = pl.multiple_of(core * 128 + CHUNK * n, CHUNK)
        half[CHUNK * n : CHUNK * (n + 1), :] = dot3(split(pair[1, pl.ds(top, CHUNK), :]), even)
        for by in (2, 3, 1):
            @pl.when(x >= by)
            def _():
                copy_x(by, n).start()

    @pl.when(core == 0)
    def _():
        odd = split(pair[1])
        tail[:, :M] = dot3(odd, even)
        tail[:, M:] = dot3(odd, h1)

    @pl.when(core == 1)
    def _():
        tail[:, :M] = pair[1]
        tail[:, M:] = h1[0].astype(F32) + h1[1].astype(F32)

    for n in range(128 // CHUNK):
        for j in range(3):
            @pl.when(x <= j)
            def _():
                arrived(j, n).wait_recv()
                pass_on(j, n).start()
    for j in range(3):
        @pl.when(x <= j)
        def _():
            for n in range(128 // CHUNK):
                passed(j, n).wait_recv()
            tail[...] = dot3(split(chips[j].reshape(M, M)), split(tail[...]))
    out_ref[0] = tail[:, :M].astype(BF16)
    out_ref[1] = tail[:, M:].astype(BF16)
    for n in range(128 // CHUNK):
        for by in (1, 2, 3):
            @pl.when(x >= by)
            def _():
                copy_x(by, n).wait_send()
        for j in range(3):
            @pl.when(x <= j)
            def _():
                pass_on(j, n).wait_send()


def smooth_kernel(ens_ref, suffix_ref, out_ref, held, sem):
    steps = held.shape[0]
    rows = held.shape[1]
    each = steps // 2

    def copy(i):
        return pltpu.make_async_copy(held.at[i], out_ref.at[i // each, pl.ds((i % each) * rows, rows)], sem.at[i])

    for i in range(steps):
        block = ens_ref[i // each, (i % each) * rows : (i % each + 1) * rows, :]
        held[i] = dot_nt(block, suffix_ref[i // each]).astype(BF16)
        copy(i).start()
    for i in range(steps):
        copy(i).wait()


def on_device(ensemble, obs_index, obs_value, obs_var):
    vmem = pl.BlockSpec(memory_space=pltpu.VMEM)
    sems = pltpu.SemaphoreType.DMA
    small = [pltpu.VMEM(a.shape, a.dtype) for a in (obs_index, obs_value, obs_var)]
    suffix, held = pl.pallas_call(
        suffix_kernel,
        out_shape=(jax.ShapeDtypeStruct((2, M, M), BF16), jax.ShapeDtypeStruct(ensemble.shape, BF16)),
        in_specs=[pl.BlockSpec(memory_space=pltpu.HBM)] * 4,
        out_specs=(vmem, vmem),
        scratch_shapes=small + [
            sems((5,)),
            pltpu.VMEM((2, 2, 8, SHARD + 8, 128), F32),
            pltpu.VMEM((2, 2, 7, SHARD + 8, 128), F32),
            pltpu.VMEM((2, 2, SHARD + 8, 128), F32),
            pltpu.VMEM((2, 2, 7, SHARD + 8, 128), F32),
            pltpu.VMEM((2, 2, 8, SHARD, 128), F32),
            pltpu.VMEM((2, 8, 128), F32),
            pltpu.VMEM((2, M, M), F32),
            pltpu.VMEM((128, M), F32),
            pltpu.VMEM((3, 2, 128, M), F32),
            pltpu.VMEM((M, 2 * M), F32),
            sems((2, 2, 7)), sems((2, 2, 7)), sems((2, 2, 7)), sems((2, 2, 7)), sems((2, 2, 7)), sems((2, 2, 7)),
            sems, sems, sems((3, 128 // CHUNK)), sems((3, 128 // CHUNK)), sems((3, 128 // CHUNK)), sems((3, 128 // CHUNK)),
        ],
        compiler_params=pltpu.CompilerParams(collective_id=0, has_side_effects=True, vmem_limit_bytes=VMEM_LIMIT),
        name="suffixes",
    )(*(pltpu.with_memory_space_constraint(a, pltpu.HBM) for a in (ensemble, obs_index, obs_value, obs_var)))
    return pl.pallas_call(
        smooth_kernel,
        out_shape=jax.ShapeDtypeStruct(ensemble.shape, BF16),
        in_specs=[vmem] * 2,
        out_specs=pl.BlockSpec(memory_space=pltpu.HBM),
        scratch_shapes=[pltpu.VMEM((8, ensemble.shape[1] // 4, M), BF16), sems((8,))],
        compiler_params=pltpu.CompilerParams(vmem_limit_bytes=VMEM_LIMIT),
        name="smooth",
    )(held, suffix)


def solution(mesh):
    placed = (P("tm", "space", None), P("tm", "space"), P("tm", "space"), P("tm", "space"))
    return jax.shard_map(
        on_device, mesh=mesh, in_specs=placed, out_specs=P("tm", "space", None), check_vma=False
    )
```

time: 55.1 us -> 52.3 us (0.949)
  Pallas kernels: 55 us -> 52.2 us
    pallas_call x1, Pallas kernels: 53.3 us -> 50.5 us  [on_device(): pl.pallas_call(suffix_kernel, out_shape=(jax.ShapeDtypeStruct((2, M, M),...]
where the time goes in v3:
time: 52.3 us; the launch traced here: 52.2 us
  Pallas kernels  52.2 us (100%)
    pallas_call x1, Pallas kernels, on_device(): pl.pallas_call(suffix_kernel, out_shape=(jax.ShapeDtypeStruct((2, M, M),...  50.5 us
    pallas_call x1, Pallas kernels, on_device(): pl.pallas_call(smooth_kernel, out_shape=jax.ShapeDtypeStruct(ensemble.sha...  1.7 us

profile of v3, /device:TPU:1, one launch (start us, length us, event | category | flops | bytes accessed | tf_op | source)
XLA Modules:
  0.0 52.2 jit_solution(4191678842639574463)
XLA Ops:
  0.0 50.5 %suffixes.1 = (bf16[2,256,256]{2,1,0:T(8,128)(2,1)S(1)}, bf16[2,2048,256]{2,1,0:T(8,128)(2,1)S(1)}) custom-call(bf16[2,2048,256]{2,1,0:T(8,128)(2,1)} %ens_in.1, s32[2,512]{1,0:T(2,128)} %index_in.1, f32[2,512]{1,0:T(2,128)} %value_in.1, f32[2,512]{1,0:T(2,128)} %var_in.1), custom_call_target="tpu_custom_call" | custom-call | tf_op jit(solution)/shard_map/suffixes/pallas_call | solution.py:354
  50.5 1.7 %smooth.1 = bf16[2,2048,256]{2,1,0:T(8,128)(2,1)} custom-call(bf16[2,2048,256]{2,1,0:T(8,128)(2,1)S(1)} %get-tuple-element.7.ens_ref, bf16[2,256,256]{2,1,0:T(8,128)(2,1)S(1)} %get-tuple-element.8.suffix_ref), custom_call_target="tpu_custom_call" | custom-call | tf_op jit(solution)/shard_map/smooth/pallas_call | solution.py:377

commit v4 on v3

--- a/solution.py
+++ b/solution.py
@@ -12,7 +12,8 @@
 BF16 = jnp.bfloat16
 ORDER = (4, 3, 5, 2, 6, 1, 7)
 SHARD = 16
-CHUNK = 64
+CHUNK = 32
+CHUNKS = 128 // CHUNK
 VMEM_LIMIT = 20 * 2**20
 
 
@@ -22,10 +23,6 @@
 
 def dot_nt(a, b):
     return lax.dot_general(a, b, (((1,), (1,)), ((), ())), preferred_element_type=F32)
-
-
-def dot_tn(a, b):
-    return lax.dot_general(a, b, (((0,), (0,)), ((), ())), preferred_element_type=F32)
 
 
 def split(a):
@@ -51,20 +48,17 @@
     rest = terms - first.astype(F32)
     second = rest.astype(BF16)
     third = (rest - second.astype(F32)).astype(BF16)
-    columns = dot_nt(at_low, first) + (dot_nt(at_low, second) + dot_nt(at_low, third))
-    rows = dot_nt(first, at_low) + (dot_nt(second, at_low) + dot_nt(third, at_low))
+    rows = dot_nt(jnp.concatenate([first, second, third], axis=1), jnp.concatenate([at_low] * 3, axis=1))
+    w_row = jnp.concatenate([rows[i : i + 1, :] for i in range(16)], axis=1)
     s_row = jnp.concatenate([rows[16 + i : 17 + i, :] for i in range(16)], axis=1)
     s_first, s_second = split(s_row)
-    return columns, jnp.concatenate([s_first, s_second, jnp.zeros((14, s_row.shape[1]), BF16)], axis=0)
-
-
-def local_sums(ens, columns, s_both):
-    scaled = [split(ens[128 * i : 128 * (i + 1), :].astype(F32) * columns[:, i : i + 1]) for i in range(16)]
-    scaled_first = jnp.concatenate([a for a, _ in scaled], axis=0)
-    scaled_second = jnp.concatenate([b for _, b in scaled], axis=0)
-    gram = dot_tn(ens, scaled_first) + dot_tn(ens, scaled_second)
+    return w_row, jnp.concatenate([s_first, s_second, jnp.zeros((14, s_row.shape[1]), BF16)], axis=0)
+
+
+def local_sums(ens, w_row, s_both):
+    first, second = split(ens.T.astype(F32) * w_row)
     proj = dot(s_both, ens)
-    return gram, proj[0:1, :] + proj[1:2, :]
+    return dot(first, ens) + dot(second, ens), proj[0:1, :] + proj[1:2, :]
 
 
 def pack(gram, proj):
@@ -101,7 +95,7 @@
     def after(a, b):
         return dot(jnp.concatenate(a, axis=1), jnp.concatenate([b, b], axis=0))
 
-    scales, projs, y, z = [], [], [], []
+    scales, projs, y, z, before = [], [], [], [], []
     for gram, proj in sums:
         col_mean = jnp.mean(gram, axis=0, keepdims=True)
         row_mean = jnp.mean(gram, axis=1, keepdims=True)
@@ -112,9 +106,13 @@
         projs.append(proj - jnp.mean(proj, axis=1, keepdims=True))
         scales.append(scale)
         b = (0.5 * start).astype(BF16)
-        y.append(1.5 * start - after(split(start), b))
+        y.append(1.5 * start - dot(start.astype(BF16), b))
         z.append(1.5 * eye - b.astype(F32))
-    for step in range(1, NS_ITERS - 1):
+        before.append(b)
+    b = [(0.5 * dot(z[w].astype(BF16), y[w].astype(BF16))).astype(BF16) for w in count]
+    z = [1.5 * z[w] - (1.5 * b[w].astype(F32) - dot(b[w], before[w])) for w in count]
+    y = [1.5 * y[w] - dot(y[w].astype(BF16), b[w]) for w in count]
+    for step in range(2, NS_ITERS - 1):
         zs, ys = [split(a) for a in z], [split(a) for a in y]
         b = [(0.5 * dot(zs[w][0], ys[w][0])).astype(BF16) for w in count]
         z = [1.5 * z[w] - twice(b[w], zs[w]) for w in count]
@@ -136,7 +134,7 @@
 def suffix_kernel(
     ens_in, index_in, value_in, var_in, out_ref, ens_ref,
     index_ref, value_ref, var_ref, load, parts, got1, mine, got2, whole, extras, pair, half, chips, tail,
-    send1, recv1, send2, recv2, send3, recv3, core_send, core_recv, x_send, x_recv, f_send, f_recv,
+    send1, recv1, send2, recv2, send3, recv3, core_send, core_recv, x_send, x_recv, f_send, f_recv, last, relay_send,
 ):
     t = lax.axis_index("tm")
     s = lax.axis_index("space")
@@ -287,10 +285,16 @@
             recv_sem=f_recv.at[j, n], device_id=sibling, device_id_type=MESH,
         )
 
-    for n in range(128 // CHUNK):
+    relay = pltpu.make_async_remote_copy(
+        src_ref=chips.at[2 - x, core, pl.ds(0, CHUNK)], dst_ref=chips.at[2 - x, core, pl.ds(0, CHUNK)],
+        send_sem=relay_send, recv_sem=x_recv.at[2 - x, 0], device_id={"tm": (1 - x) * 2 + core, "space": s},
+        device_id_type=MESH,
+    )
+
+    for n in range(CHUNKS):
         top = pl.multiple_of(core * 128 + CHUNK * n, CHUNK)
         half[CHUNK * n : CHUNK * (n + 1), :] = dot3(split(pair[1, pl.ds(top, CHUNK), :]), even)
-        for by in (2, 3, 1):
+        for by in (2, 3, 1) if n else (3, 1):
             @pl.when(x >= by)
             def _():
                 copy_x(by, n).start()
@@ -306,22 +310,64 @@
         tail[:, :M] = pair[1]
         tail[:, M:] = h1[0].astype(F32) + h1[1].astype(F32)
 
-    for n in range(128 // CHUNK):
-        for j in range(3):
-            @pl.when(x <= j)
-            def _():
-                arrived(j, n).wait_recv()
-                pass_on(j, n).start()
-    for j in range(3):
-        @pl.when(x <= j)
+    def receive(by, n):
+        @pl.when(x + by <= 3)
         def _():
-            for n in range(128 // CHUNK):
-                passed(j, n).wait_recv()
-            tail[...] = dot3(split(chips[j].reshape(M, M)), split(tail[...]))
+            arrived(x + by - 1, n).wait_recv()
+            pass_on(x + by - 1, n).start()
+
+    receive(1, 0)
+    receive(3, 0)
+
+    @pl.when(x <= 1)
+    def _():
+        relay.start()
+
+    for n in range(1, CHUNKS):
+        for by in (1, 3, 2):
+            receive(by, n)
+    receive(2, 0)
+
+    def chip(j):
+        for n in range(CHUNKS):
+            passed(j, n).wait_recv()
+        return split(chips[j].reshape(M, M))
+
+    @pl.when(x == 0)
+    def _():
+        tail[...] = dot3(chip(0), split(tail[...]))
+
+    @pl.when(x <= 1)
+    def _():
+        first = chip(1)
+
+        @pl.when(x == 0)
+        def _():
+            last[...] = dot3(chip(2), first)
+
+        @pl.when(x == 1)
+        def _():
+            tail[...] = dot3(first, split(tail[...]))
+
+    @pl.when((x == 1) | (x == 2))
+    def _():
+        for n in range(CHUNKS):
+            passed(2, n).wait_recv()
+        last[...] = chips[2].reshape(M, M)
+
+    @pl.when(x <= 2)
+    def _():
+        tail[...] = dot3(split(last[...]), split(tail[...]))
+
     out_ref[0] = tail[:, :M].astype(BF16)
     out_ref[1] = tail[:, M:].astype(BF16)
-    for n in range(128 // CHUNK):
-        for by in (1, 2, 3):
+
+    @pl.when(x <= 1)
+    def _():
+        relay.wait_send()
+
+    for n in range(CHUNKS):
+        for by in (1, 2, 3) if n else (1, 3):
             @pl.when(x >= by)
             def _():
                 copy_x(by, n).wait_send()
@@ -369,7 +415,8 @@
             pltpu.VMEM((3, 2, 128, M), F32),
             pltpu.VMEM((M, 2 * M), F32),
             sems((2, 2, 7)), sems((2, 2, 7)), sems((2, 2, 7)), sems((2, 2, 7)), sems((2, 2, 7)), sems((2, 2, 7)),
-            sems, sems, sems((3, 128 // CHUNK)), sems((3, 128 // CHUNK)), sems((3, 128 // CHUNK)), sems((3, 128 // CHUNK)),
+            sems, sems, sems((3, CHUNKS)), sems((3, CHUNKS)), sems((3, CHUNKS)), sems((3, CHUNKS)),
+            pltpu.VMEM((M, M), F32), sems,
         ],
         compiler_params=pltpu.CompilerParams(collective_id=0, has_side_effects=True, vmem_limit_bytes=VMEM_LIMIT),
         name="suffixes",

time: 52.3 us -> 51.8 us (level)
  no operation moved by 1% of the time
where the time goes in v4:
time: 51.8 us; the launch traced here: 51.7 us
  Pallas kernels  51.7 us (100%)
    pallas_call x1, Pallas kernels, on_device(): pl.pallas_call(suffix_kernel, out_shape=(jax.ShapeDtypeStruct((2, M, M),...  50 us
    pallas_call x1, Pallas kernels, on_device(): pl.pallas_call(smooth_kernel, out_shape=jax.ShapeDtypeStruct(ensemble.sha...  1.71 us

profile of v4, /device:TPU:1, one launch (start us, length us, event | category | flops | bytes accessed | tf_op | source)
XLA Modules:
  0.0 51.7 jit_solution(8912246770670800649)
XLA Ops:
  0.0 50.0 %suffixes.1 = (bf16[2,256,256]{2,1,0:T(8,128)(2,1)S(1)}, bf16[2,2048,256]{2,1,0:T(8,128)(2,1)S(1)}) custom-call(bf16[2,2048,256]{2,1,0:T(8,128)(2,1)} %ens_in.1, s32[2,512]{1,0:T(2,128)} %index_in.1, f32[2,512]{1,0:T(2,128)} %value_in.1, f32[2,512]{1,0:T(2,128)} %var_in.1), custom_call_target="tpu_custom_call" | custom-call | tf_op jit(solution)/shard_map/suffixes/pallas_call | solution.py:400
  50.0 1.7 %smooth.1 = bf16[2,2048,256]{2,1,0:T(8,128)(2,1)} custom-call(bf16[2,2048,256]{2,1,0:T(8,128)(2,1)S(1)} %get-tuple-element.7.ens_ref, bf16[2,256,256]{2,1,0:T(8,128)(2,1)S(1)} %get-tuple-element.8.suffix_ref), custom_call_target="tpu_custom_call" | custom-call | tf_op jit(solution)/shard_map/smooth/pallas_call | solution.py:424

commit v5 on v4

--- a/solution.py
+++ b/solution.py
@@ -14,6 +14,7 @@
 SHARD = 16
 CHUNK = 32
 CHUNKS = 128 // CHUNK
+RELAYED = 2
 VMEM_LIMIT = 20 * 2**20
 
 
@@ -135,6 +136,7 @@
     ens_in, index_in, value_in, var_in, out_ref, ens_ref,
     index_ref, value_ref, var_ref, load, parts, got1, mine, got2, whole, extras, pair, half, chips, tail,
     send1, recv1, send2, recv2, send3, recv3, core_send, core_recv, x_send, x_recv, f_send, f_recv, last, relay_send,
+    ext1, ext_mine, ext2, ext_all, ext_send, ext_recv1, ext_recv2, ext_recv3,
 ):
     t = lax.axis_index("tm")
     s = lax.axis_index("space")
@@ -170,19 +172,16 @@
     def axis_of(w, p):
         return (w + p) % 2
 
-    def sent(p):
-        return pl.ds(0, SHARD + 8 * p)
-
     def copy1(w, p, i):
         axis, by = axis_of(w, p), ORDER[i]
         return pltpu.make_async_remote_copy(
-            src_ref=parts.at[w, p, (at[axis] + by) % 8, sent(p)], dst_ref=got1.at[w, p, i, sent(p)],
+            src_ref=parts.at[w, p, (at[axis] + by) % 8], dst_ref=got1.at[w, p, i],
             send_sem=send1.at[w, p, i], recv_sem=recv1.at[w, p, i], device_id=along(axis, by), device_id_type=MESH,
         )
 
     def copy2(w, p, i):
         return pltpu.make_async_remote_copy(
-            src_ref=mine.at[w, p, sent(p)], dst_ref=got2.at[w, p, i, sent(p)],
+            src_ref=mine.at[w, p], dst_ref=got2.at[w, p, i],
             send_sem=send2.at[w, p, i], recv_sem=recv2.at[w, p, i],
             device_id=along(1 - axis_of(w, p), ORDER[i]), device_id_type=MESH,
         )
@@ -192,6 +191,34 @@
         return pltpu.make_async_remote_copy(
             src_ref=whole.at[w, p, at[axis]], dst_ref=whole.at[w, p, at[axis]],
             send_sem=send3.at[w, p, i], recv_sem=recv3.at[w, p, i], device_id=along(axis, ORDER[i]), device_id_type=MESH,
+        )
+
+    def first_on(w):
+        return at[axis_of(w, 1)] == 0
+
+    def extra1(w):
+        axis = axis_of(w, 1)
+        return pltpu.make_async_remote_copy(
+            src_ref=extras.at[w], dst_ref=ext1.at[w, at[axis] - 1], send_sem=ext_send.at[w, 0],
+            recv_sem=ext_recv1.at[w, at[axis] - 1], device_id=along(axis, 8 - at[axis]), device_id_type=MESH,
+        )
+
+    def extra1_here(w, i):
+        return pltpu.make_async_remote_copy(
+            src_ref=extras.at[w], dst_ref=ext1.at[w, i], send_sem=ext_send.at[w, 0],
+            recv_sem=ext_recv1.at[w, i], device_id=along(axis_of(w, 1), 1), device_id_type=MESH,
+        )
+
+    def extra2(w, i):
+        return pltpu.make_async_remote_copy(
+            src_ref=ext_mine.at[w], dst_ref=ext2.at[w, i], send_sem=ext_send.at[w, 1 + i],
+            recv_sem=ext_recv2.at[w, i], device_id=along(1 - axis_of(w, 1), ORDER[i]), device_id_type=MESH,
+        )
+
+    def extra3(w, i):
+        return pltpu.make_async_remote_copy(
+            src_ref=ext_all.at[w], dst_ref=ext_all.at[w], send_sem=ext_send.at[w, 8 + i],
+            recv_sem=ext_recv3.at[w], device_id=along(axis_of(w, 1), ORDER[i]), device_id_type=MESH,
         )
 
     for copy in loads[:3]:
@@ -200,35 +227,56 @@
     for w in range(2):
         loads[3 + w].wait()
         k12, mixed, extra = pack(*local_sums(ens_ref[w], *sums[w]))
-        for k in range(8):
-            parts[w, 0, k, 0:SHARD, :] = k12[SHARD * k : SHARD * (k + 1), :]
-            parts[w, 1, k, 0:SHARD, :] = mixed[SHARD * k : SHARD * (k + 1), :]
-            parts[w, 1, k, SHARD:, :] = extra
-        if w == 0:
-            pl.semaphore_wait(barrier, 18)
+        parts[w, 0] = k12.reshape(8, SHARD, 128)
+        parts[w, 1] = mixed.reshape(8, SHARD, 128)
+        extras[w] = extra
+    pl.semaphore_wait(barrier, 18)
+    for w in range(2):
         for i in range(7):
             for p in range(2):
                 copy1(w, p, i).start()
 
+        @pl.when(~first_on(w))
+        def _():
+            extra1(w).start()
+
     for w, p in blocks:
-        total = parts[w, p, at[axis_of(w, p)], sent(p)]
+        total = parts[w, p, at[axis_of(w, p)]]
         for i in range(7):
             copy1(w, p, i).wait_recv()
-            total = total + got1[w, p, i, sent(p)]
-        mine[w, p, sent(p)] = total
+            total = total + got1[w, p, i]
+        mine[w, p] = total
         for i in range(7):
             copy2(w, p, i).start()
+        if p == 1:
+            @pl.when(first_on(w))
+            def _():
+                total = extras[w]
+                for i in range(7):
+                    extra1_here(w, i).wait_recv()
+                    total = total + ext1[w, i]
+                ext_mine[w] = total
+                for i in range(7):
+                    extra2(w, i).start()
 
     for w, p in blocks:
-        total = mine[w, p, sent(p)]
+        total = mine[w, p]
         for i in range(7):
             copy2(w, p, i).wait_recv()
-            total = total + got2[w, p, i, sent(p)]
-        whole[w, p, at[axis_of(w, p)]] = total[:SHARD]
+            total = total + got2[w, p, i]
+        whole[w, p, at[axis_of(w, p)]] = total
+        for i in range(7):
+            copy3(w, p, i).start()
         if p == 1:
-            extras[w] = total[SHARD:]
-        for i in range(7):
-            copy3(w, p, i).start()
+            @pl.when(first_on(w))
+            def _():
+                total = ext_mine[w]
+                for i in range(7):
+                    extra2(w, i).wait_recv()
+                    total = total + ext2[w, i]
+                ext_all[w] = total
+                for i in range(7):
+                    extra3(w, i).start()
 
     for w, p in blocks:
         for i in range(7):
@@ -236,25 +284,48 @@
     for w, p in blocks:
         for i in range(7):
             copy3(w, p, i).wait_recv()
+    for w in range(2):
+        @pl.when(~first_on(w))
+        def _():
+            extra3(w, 0).wait_recv()
 
     h0, h1 = transforms(
-        [unpack(whole[w, 0].reshape(128, 128), whole[w, 1].reshape(128, 128), extras[w]) for w in range(2)]
+        [unpack(whole[w, 0].reshape(128, 128), whole[w, 1].reshape(128, 128), ext_all[w]) for w in range(2)]
     )
     h0, h1 = split(h0), split(h1)
     own = dot3(h1, h0)
     pair[core] = own
-    swap = pltpu.make_async_remote_copy(
-        src_ref=pair.at[core], dst_ref=pair.at[core], send_sem=core_send, recv_sem=core_recv,
-        device_id=sibling, device_id_type=MESH,
-    )
-    swap.start()
+
+    def swap(n):
+        rows = pl.ds(128 * n, 128)
+        return pltpu.make_async_remote_copy(
+            src_ref=pair.at[core, rows], dst_ref=pair.at[core, rows], send_sem=core_send.at[n], recv_sem=core_recv.at[n],
+            device_id=sibling, device_id_type=MESH,
+        )
+
+    swap(0).start()
+    swap(1).start()
     for w, p in blocks:
         for i in range(7):
             copy2(w, p, i).wait_send()
-    for w, p in blocks:
-        for i in range(7):
             copy3(w, p, i).wait_send()
-    swap.wait()
+    for w in range(2):
+        @pl.when(first_on(w))
+        def _():
+            for i in range(7):
+                extra2(w, i).wait_send()
+                extra3(w, i).wait_send()
+
+        @pl.when(~first_on(w))
+        def _():
+            extra1(w).wait_send()
+
+    swap(0).wait_recv()
+
+    @pl.when(core == 1)
+    def _():
+        swap(1).wait_recv()
+
     even = split(pair[0])
 
     def copy_x(by, n):
@@ -285,22 +356,24 @@
             recv_sem=f_recv.at[j, n], device_id=sibling, device_id_type=MESH,
         )
 
-    relay = pltpu.make_async_remote_copy(
-        src_ref=chips.at[2 - x, core, pl.ds(0, CHUNK)], dst_ref=chips.at[2 - x, core, pl.ds(0, CHUNK)],
-        send_sem=relay_send, recv_sem=x_recv.at[2 - x, 0], device_id={"tm": (1 - x) * 2 + core, "space": s},
-        device_id_type=MESH,
-    )
+    def relay(n):
+        rows = pl.ds(CHUNK * n, CHUNK)
+        return pltpu.make_async_remote_copy(
+            src_ref=chips.at[2 - x, core, rows], dst_ref=chips.at[2 - x, core, rows], send_sem=relay_send.at[n],
+            recv_sem=x_recv.at[2 - x, n], device_id={"tm": (1 - x) * 2 + core, "space": s}, device_id_type=MESH,
+        )
 
     for n in range(CHUNKS):
         top = pl.multiple_of(core * 128 + CHUNK * n, CHUNK)
         half[CHUNK * n : CHUNK * (n + 1), :] = dot3(split(pair[1, pl.ds(top, CHUNK), :]), even)
-        for by in (2, 3, 1) if n else (3, 1):
+        for by in (2, 3, 1) if n >= RELAYED else (3, 1):
             @pl.when(x >= by)
             def _():
                 copy_x(by, n).start()
 
     @pl.when(core == 0)
     def _():
+        swap(1).wait_recv()
         odd = split(pair[1])
         tail[:, :M] = dot3(odd, even)
         tail[:, M:] = dot3(odd, h1)
@@ -316,17 +389,17 @@
             arrived(x + by - 1, n).wait_recv()
             pass_on(x + by - 1, n).start()
 
-    receive(1, 0)
-    receive(3, 0)
-
-    @pl.when(x <= 1)
-    def _():
-        relay.start()
-
-    for n in range(1, CHUNKS):
-        for by in (1, 3, 2):
-            receive(by, n)
-    receive(2, 0)
+    for n in range(CHUNKS):
+        receive(1, n)
+        receive(3, n)
+        if n < RELAYED:
+            @pl.when(x <= 1)
+            def _():
+                relay(n).start()
+        else:
+            receive(2, n)
+    for n in range(RELAYED):
+        receive(2, n)
 
     def chip(j):
         for n in range(CHUNKS):
@@ -364,10 +437,13 @@
 
     @pl.when(x <= 1)
     def _():
-        relay.wait_send()
-
+        for n in range(RELAYED):
+            relay(n).wait_send()
+
+    for n in range(2):
+        swap(n).wait_send()
     for n in range(CHUNKS):
-        for by in (1, 2, 3) if n else (1, 3):
+        for by in (1, 2, 3) if n >= RELAYED else (1, 3):
             @pl.when(x >= by)
             def _():
                 copy_x(by, n).wait_send()
@@ -404,10 +480,10 @@
         out_specs=(vmem, vmem),
         scratch_shapes=small + [
             sems((5,)),
-            pltpu.VMEM((2, 2, 8, SHARD + 8, 128), F32),
-            pltpu.VMEM((2, 2, 7, SHARD + 8, 128), F32),
-            pltpu.VMEM((2, 2, SHARD + 8, 128), F32),
-            pltpu.VMEM((2, 2, 7, SHARD + 8, 128), F32),
+            pltpu.VMEM((2, 2, 8, SHARD, 128), F32),
+            pltpu.VMEM((2, 2, 7, SHARD, 128), F32),
+            pltpu.VMEM((2, 2, SHARD, 128), F32),
+            pltpu.VMEM((2, 2, 7, SHARD, 128), F32),
             pltpu.VMEM((2, 2, 8, SHARD, 128), F32),
             pltpu.VMEM((2, 8, 128), F32),
             pltpu.VMEM((2, M, M), F32),
@@ -415,8 +491,11 @@
             pltpu.VMEM((3, 2, 128, M), F32),
             pltpu.VMEM((M, 2 * M), F32),
             sems((2, 2, 7)), sems((2, 2, 7)), sems((2, 2, 7)), sems((2, 2, 7)), sems((2, 2, 7)), sems((2, 2, 7)),
-            sems, sems, sems((3, CHUNKS)), sems((3, CHUNKS)), sems((3, CHUNKS)), sems((3, CHUNKS)),
-            pltpu.VMEM((M, M), F32), sems,
+            sems((2,)), sems((2,)), sems((3, CHUNKS)), sems((3, CHUNKS)), sems((3, CHUNKS)), sems((3, CHUNKS)),
+            pltpu.VMEM((M, M), F32), sems((RELAYED,)),
+            pltpu.VMEM((2, 7, 8, 128), F32), pltpu.VMEM((2, 8, 128), F32),
+            pltpu.VMEM((2, 7, 8, 128), F32), pltpu.VMEM((2, 8, 128), F32),
+            sems((2, 15)), sems((2, 7)), sems((2, 7)), sems((2,)),
         ],
         compiler_params=pltpu.CompilerParams(collective_id=0, has_side_effects=True, vmem_limit_bytes=VMEM_LIMIT),
         name="suffixes",

time: 51.8 us -> 49.8 us (0.961)
  Pallas kernels: 51.7 us -> 49.7 us
    pallas_call x1, Pallas kernels: 50 us -> 48 us  [on_device(): pl.pallas_call(suffix_kernel, out_shape=(jax.ShapeDtypeStruct((2, M, M),...]
where the time goes in v5:
time: 49.8 us; the launch traced here: 49.7 us
  Pallas kernels  49.7 us (100%)
    pallas_call x1, Pallas kernels, on_device(): pl.pallas_call(suffix_kernel, out_shape=(jax.ShapeDtypeStruct((2, M, M),...  48 us
    pallas_call x1, Pallas kernels, on_device(): pl.pallas_call(smooth_kernel, out_shape=jax.ShapeDtypeStruct(ensemble.sha...  1.71 us

profile of v5, /device:TPU:1, one launch (start us, length us, event | category | flops | bytes accessed | tf_op | source)
XLA Modules:
  0.0 49.7 jit_solution(6209641726679497941)
XLA Ops:
  0.0 48.0 %suffixes.1 = (bf16[2,256,256]{2,1,0:T(8,128)(2,1)S(1)}, bf16[2,2048,256]{2,1,0:T(8,128)(2,1)S(1)}) custom-call(bf16[2,2048,256]{2,1,0:T(8,128)(2,1)} %ens_in.1, s32[2,512]{1,0:T(2,128)} %index_in.1, f32[2,512]{1,0:T(2,128)} %value_in.1, f32[2,512]{1,0:T(2,128)} %var_in.1), custom_call_target="tpu_custom_call" | custom-call | tf_op jit(solution)/shard_map/suffixes/pallas_call | solution.py:476
  48.0 1.7 %smooth.1 = bf16[2,2048,256]{2,1,0:T(8,128)(2,1)} custom-call(bf16[2,2048,256]{2,1,0:T(8,128)(2,1)S(1)} %get-tuple-element.7.ens_ref, bf16[2,256,256]{2,1,0:T(8,128)(2,1)S(1)} %get-tuple-element.8.suffix_ref), custom_call_target="tpu_custom_call" | custom-call | tf_op jit(solution)/shard_map/smooth/pallas_call | solution.py:503

commit v6 on v5

--- a/solution.py
+++ b/solution.py
@@ -84,11 +84,29 @@
     return gram, jnp.concatenate([extra[1:2, :], extra[2:3, :]], axis=1)
 
 
-def transforms(sums):
+def identity():
     r = lax.broadcasted_iota(jnp.int32, (M, M), 0)
     c = lax.broadcasted_iota(jnp.int32, (M, M), 1)
-    eye = jnp.where(r == c, 1.0, 0.0).astype(F32)
-    count = range(len(sums))
+    return jnp.where(r == c, 1.0, 0.0).astype(F32)
+
+
+def begin(gram, proj):
+    eye = identity()
+    col_mean = jnp.mean(gram, axis=0, keepdims=True)
+    row_mean = jnp.mean(gram, axis=1, keepdims=True)
+    amat = gram - row_mean - (col_mean - jnp.mean(col_mean, axis=1, keepdims=True)) + (M - 1.0) * eye
+    scale = jnp.sqrt(jnp.sum(jnp.sum(amat * amat, axis=0, keepdims=True), axis=1, keepdims=True))
+    start = amat * (1.0 / scale)
+    proj = proj - col_mean
+    proj = proj - jnp.mean(proj, axis=1, keepdims=True)
+    b = (0.5 * start).astype(BF16)
+    return scale, proj, 1.5 * start - dot(start.astype(BF16), b), 1.5 * eye - b.astype(F32), b
+
+
+def transforms(begun):
+    eye = identity()
+    count = range(len(begun))
+    scales, projs, y, z, before = (list(a) for a in zip(*begun))
 
     def twice(a, b):
         return dot(jnp.concatenate([a, a], axis=1), jnp.concatenate(b, axis=0))
@@ -96,20 +114,6 @@
     def after(a, b):
         return dot(jnp.concatenate(a, axis=1), jnp.concatenate([b, b], axis=0))
 
-    scales, projs, y, z, before = [], [], [], [], []
-    for gram, proj in sums:
-        col_mean = jnp.mean(gram, axis=0, keepdims=True)
-        row_mean = jnp.mean(gram, axis=1, keepdims=True)
-        amat = gram - row_mean - (col_mean - jnp.mean(col_mean, axis=1, keepdims=True)) + (M - 1.0) * eye
-        scale = jnp.sqrt(jnp.sum(jnp.sum(amat * amat, axis=0, keepdims=True), axis=1, keepdims=True))
-        start = amat * (1.0 / scale)
-        proj = proj - col_mean
-        projs.append(proj - jnp.mean(proj, axis=1, keepdims=True))
-        scales.append(scale)
-        b = (0.5 * start).astype(BF16)
-        y.append(1.5 * start - dot(start.astype(BF16), b))
-        z.append(1.5 * eye - b.astype(F32))
-        before.append(b)
     b = [(0.5 * dot(z[w].astype(BF16), y[w].astype(BF16))).astype(BF16) for w in count]
     z = [1.5 * z[w] - (1.5 * b[w].astype(F32) - dot(b[w], before[w])) for w in count]
     y = [1.5 * y[w] - dot(y[w].astype(BF16), b[w]) for w in count]
@@ -135,8 +139,8 @@
 def suffix_kernel(
     ens_in, index_in, value_in, var_in, out_ref, ens_ref,
     index_ref, value_ref, var_ref, load, parts, got1, mine, got2, whole, extras, pair, half, chips, tail,
-    send1, recv1, send2, recv2, send3, recv3, core_send, core_recv, x_send, x_recv, f_send, f_recv, last, relay_send,
-    ext1, ext_mine, ext2, ext_all, ext_send, ext_recv1, ext_recv2, ext_recv3,
+    send_1, recv1, send2, recv2, send3, recv3, core_send, core_recv, x_send, x_recv, f_send, f_recv, last, relay_send,
+    ext1, ext_mine, ext2, ext_all, ext_send, ext_recv1, ext_recv2, ext_recv3, ready,
 ):
     t = lax.axis_index("tm")
     s = lax.axis_index("space")
@@ -162,9 +166,11 @@
     barrier = pltpu.get_barrier_semaphore()
     for by in ORDER:
         for axis in range(2):
-            pl.semaphore_signal(barrier, inc=1, device_id=along(axis, by), device_id_type=MESH)
+            there = {"tm": x * 2 + axis, "space": along(axis, by)["space"]}
+            pl.semaphore_signal(barrier, inc=1, device_id=there, device_id_type=MESH)
     for by in (1, 2, 3):
-        pl.semaphore_signal(barrier, inc=1, device_id=on_x(by), device_id_type=MESH)
+        there = {"tm": ((x + by) % 4) * 2, "space": s}
+        pl.semaphore_signal(barrier, inc=1, device_id=there, device_id_type=MESH)
     pl.semaphore_signal(barrier, inc=1, device_id=sibling, device_id_type=MESH)
 
     blocks = [(w, p) for w in range(2) for p in range(2)]
@@ -176,7 +182,7 @@
         axis, by = axis_of(w, p), ORDER[i]
         return pltpu.make_async_remote_copy(
             src_ref=parts.at[w, p, (at[axis] + by) % 8], dst_ref=got1.at[w, p, i],
-            send_sem=send1.at[w, p, i], recv_sem=recv1.at[w, p, i], device_id=along(axis, by), device_id_type=MESH,
+            send_sem=send_1.at[w, p, i], recv_sem=recv1.at[w, p, i], device_id=along(axis, by), device_id_type=MESH,
         )
 
     def copy2(w, p, i):
@@ -230,15 +236,30 @@
         parts[w, 0] = k12.reshape(8, SHARD, 128)
         parts[w, 1] = mixed.reshape(8, SHARD, 128)
         extras[w] = extra
-    pl.semaphore_wait(barrier, 18)
-    for w in range(2):
-        for i in range(7):
-            for p in range(2):
+    def send1(axis):
+        for w in range(2):
+            p = (axis + w) % 2
+            for i in range(7):
                 copy1(w, p, i).start()
-
-        @pl.when(~first_on(w))
-        def _():
-            extra1(w).start()
+            if p == 1:
+                @pl.when(~first_on(w))
+                def _():
+                    extra1(w).start()
+
+    pl.semaphore_wait(barrier, jnp.where(core == 0, 21, 15))
+    pl.semaphore_signal(ready, inc=1, device_id=sibling, device_id_type=MESH)
+
+    @pl.when(core == 0)
+    def _():
+        send1(0)
+        pl.semaphore_wait(ready, 1)
+        send1(1)
+
+    @pl.when(core == 1)
+    def _():
+        send1(1)
+        pl.semaphore_wait(ready, 1)
+        send1(0)
 
     for w, p in blocks:
         total = parts[w, p, at[axis_of(w, p)]]
@@ -281,20 +302,19 @@
     for w, p in blocks:
         for i in range(7):
             copy1(w, p, i).wait_send()
-    for w, p in blocks:
-        for i in range(7):
-            copy3(w, p, i).wait_recv()
+    begun = []
     for w in range(2):
+        for p in range(2):
+            for i in range(7):
+                copy3(w, p, i).wait_recv()
+
         @pl.when(~first_on(w))
         def _():
             extra3(w, 0).wait_recv()
 
-    h0, h1 = transforms(
-        [unpack(whole[w, 0].reshape(128, 128), whole[w, 1].reshape(128, 128), ext_all[w]) for w in range(2)]
-    )
+        begun.append(begin(*unpack(whole[w, 0].reshape(128, 128), whole[w, 1].reshape(128, 128), ext_all[w])))
+    h0, h1 = transforms(begun)
     h0, h1 = split(h0), split(h1)
-    own = dot3(h1, h0)
-    pair[core] = own
 
     def swap(n):
         rows = pl.ds(128 * n, 128)
@@ -303,8 +323,10 @@
             device_id=sibling, device_id_type=MESH,
         )
 
-    swap(0).start()
-    swap(1).start()
+    for n in range(2):
+        rows = slice(128 * n, 128 * (n + 1))
+        pair[core, rows] = dot3((h1[0][rows], h1[1][rows]), h0)
+        swap(n).start()
     for w, p in blocks:
         for i in range(7):
             copy2(w, p, i).wait_send()
@@ -495,7 +517,7 @@
             pltpu.VMEM((M, M), F32), sems((RELAYED,)),
             pltpu.VMEM((2, 7, 8, 128), F32), pltpu.VMEM((2, 8, 128), F32),
             pltpu.VMEM((2, 7, 8, 128), F32), pltpu.VMEM((2, 8, 128), F32),
-            sems((2, 15)), sems((2, 7)), sems((2, 7)), sems((2,)),
+            sems((2, 15)), sems((2, 7)), sems((2, 7)), sems((2,)), pltpu.SemaphoreType.REGULAR,
         ],
         compiler_params=pltpu.CompilerParams(collective_id=0, has_side_effects=True, vmem_limit_bytes=VMEM_LIMIT),
         name="suffixes",

time: 49.8 us -> 49.5 us (level)
  no operation moved by 1% of the time
where the time goes in v6:
time: 49.5 us; the launch traced here: 49.3 us
  Pallas kernels  49.3 us (100%)
    pallas_call x1, Pallas kernels, on_device(): pl.pallas_call(suffix_kernel, out_shape=(jax.ShapeDtypeStruct((2, M, M),...  47.5 us
    pallas_call x1, Pallas kernels, on_device(): pl.pallas_call(smooth_kernel, out_shape=jax.ShapeDtypeStruct(ensemble.sha...  1.71 us

profile of v6, /device:TPU:1, one launch (start us, length us, event | category | flops | bytes accessed | tf_op | source)
XLA Modules:
  0.0 49.3 jit_solution(1231216426697919908)
XLA Ops:
  0.0 47.5 %suffixes.1 = (bf16[2,256,256]{2,1,0:T(8,128)(2,1)S(1)}, bf16[2,2048,256]{2,1,0:T(8,128)(2,1)S(1)}) custom-call(bf16[2,2048,256]{2,1,0:T(8,128)(2,1)} %ens_in.1, s32[2,512]{1,0:T(2,128)} %index_in.1, f32[2,512]{1,0:T(2,128)} %value_in.1, f32[2,512]{1,0:T(2,128)} %var_in.1), custom_call_target="tpu_custom_call" | custom-call | tf_op jit(solution)/shard_map/suffixes/pallas_call | solution.py:498
  47.5 1.7 %smooth.1 = bf16[2,2048,256]{2,1,0:T(8,128)(2,1)} custom-call(bf16[2,2048,256]{2,1,0:T(8,128)(2,1)S(1)} %get-tuple-element.7.ens_ref, bf16[2,256,256]{2,1,0:T(8,128)(2,1)S(1)} %get-tuple-element.8.suffix_ref), custom_call_target="tpu_custom_call" | custom-call | tf_op jit(solution)/shard_map/smooth/pallas_call | solution.py:525

commit v7 on v6

--- a/solution.py
+++ b/solution.py
@@ -139,7 +139,7 @@
 def suffix_kernel(
     ens_in, index_in, value_in, var_in, out_ref, ens_ref,
     index_ref, value_ref, var_ref, load, parts, got1, mine, got2, whole, extras, pair, half, chips, tail,
-    send_1, recv1, send2, recv2, send3, recv3, core_send, core_recv, x_send, x_recv, f_send, f_recv, last, relay_send,
+    send_1, recv1, send2, recv2, send3, recv3, core_send, core_recv, x_send, x_recv, f_send, f_recv, relay_send,
     ext1, ext_mine, ext2, ext_all, ext_send, ext_recv1, ext_recv2, ext_recv3, ready,
 ):
     t = lax.axis_index("tm")
@@ -423,36 +423,33 @@
     for n in range(RELAYED):
         receive(2, n)
 
-    def chip(j):
+    def whole_chip(j):
         for n in range(CHUNKS):
             passed(j, n).wait_recv()
-        return split(chips[j].reshape(M, M))
+        tail[...] = dot3(split(chips[j].reshape(M, M)), split(tail[...]))
+
+    def by_chunks(j):
+        right = split(tail[...])
+        for n in [*range(RELAYED, CHUNKS), *range(RELAYED)]:
+            passed(j, n).wait_recv()
+            rows = slice(CHUNK * n, CHUNK * (n + 1))
+            done = dot3(split(chips[j, :, rows].reshape(2 * CHUNK, M)), right)
+            for h in range(2):
+                tail[128 * h + CHUNK * n : 128 * h + CHUNK * (n + 1)] = done[CHUNK * h : CHUNK * (h + 1)]
 
     @pl.when(x == 0)
     def _():
-        tail[...] = dot3(chip(0), split(tail[...]))
-
-    @pl.when(x <= 1)
-    def _():
-        first = chip(1)
-
-        @pl.when(x == 0)
-        def _():
-            last[...] = dot3(chip(2), first)
-
-        @pl.when(x == 1)
-        def _():
-            tail[...] = dot3(first, split(tail[...]))
+        whole_chip(0)
+        by_chunks(1)
+        whole_chip(2)
+
+    @pl.when(x == 1)
+    def _():
+        whole_chip(1)
 
     @pl.when((x == 1) | (x == 2))
     def _():
-        for n in range(CHUNKS):
-            passed(2, n).wait_recv()
-        last[...] = chips[2].reshape(M, M)
-
-    @pl.when(x <= 2)
-    def _():
-        tail[...] = dot3(split(last[...]), split(tail[...]))
+        by_chunks(2)
 
     out_ref[0] = tail[:, :M].astype(BF16)
     out_ref[1] = tail[:, M:].astype(BF16)
@@ -514,7 +511,7 @@
             pltpu.VMEM((M, 2 * M), F32),
             sems((2, 2, 7)), sems((2, 2, 7)), sems((2, 2, 7)), sems((2, 2, 7)), sems((2, 2, 7)), sems((2, 2, 7)),
             sems((2,)), sems((2,)), sems((3, CHUNKS)), sems((3, CHUNKS)), sems((3, CHUNKS)), sems((3, CHUNKS)),
-            pltpu.VMEM((M, M), F32), sems((RELAYED,)),
+            sems((RELAYED,)),
             pltpu.VMEM((2, 7, 8, 128), F32), pltpu.VMEM((2, 8, 128), F32),
             pltpu.VMEM((2, 7, 8, 128), F32), pltpu.VMEM((2, 8, 128), F32),
             sems((2, 15)), sems((2, 7)), sems((2, 7)), sems((2,)), pltpu.SemaphoreType.REGULAR,

time: 49.5 us -> 49.8 us (level)
  no operation moved by 1% of the time
where the time goes in v7:
time: 49.8 us; the launch traced here: 49.6 us
  Pallas kernels  49.6 us (100%)
    pallas_call x1, Pallas kernels, on_device(): pl.pallas_call(suffix_kernel, out_shape=(jax.ShapeDtypeStruct((2, M, M),...  47.9 us
    pallas_call x1, Pallas kernels, on_device(): pl.pallas_call(smooth_kernel, out_shape=jax.ShapeDtypeStruct(ensemble.sha...  1.71 us

profile of v7, /device:TPU:1, one launch (start us, length us, event | category | flops | bytes accessed | tf_op | source)
XLA Modules:
  0.0 49.6 jit_solution(14063445371394757322)
XLA Ops:
  0.0 47.9 %suffixes.1 = (bf16[2,256,256]{2,1,0:T(8,128)(2,1)S(1)}, bf16[2,2048,256]{2,1,0:T(8,128)(2,1)S(1)}) custom-call(bf16[2,2048,256]{2,1,0:T(8,128)(2,1)} %ens_in.1, s32[2,512]{1,0:T(2,128)} %index_in.1, f32[2,512]{1,0:T(2,128)} %value_in.1, f32[2,512]{1,0:T(2,128)} %var_in.1), custom_call_target="tpu_custom_call" | custom-call | tf_op jit(solution)/shard_map/suffixes/pallas_call | solution.py:495
  47.9 1.7 %smooth.1 = bf16[2,2048,256]{2,1,0:T(8,128)(2,1)} custom-call(bf16[2,2048,256]{2,1,0:T(8,128)(2,1)S(1)} %get-tuple-element.7.ens_ref, bf16[2,256,256]{2,1,0:T(8,128)(2,1)S(1)} %get-tuple-element.8.suffix_ref), custom_call_target="tpu_custom_call" | custom-call | tf_op jit(solution)/shard_map/smooth/pallas_call | solution.py:522
